TPU v7x, 512 devices: a whole 4x8x8 slice. The times are simulated.
512 devices in a mesh: row: 32 (over x_lo, y, core), col: 16 (over x_hi, z).
Axes of the slice: x: 4 (x_hi: 2, x_lo: 2; x = x_hi * 2 + x_lo), y: 8, z: 8, core: 2. Of those that a mesh axis runs over, the one named last changes fastest.
Arguments:
- observed: float32 [1, 4096, 8192], P(None, 'row', 'col'), may hold values from 0.2 to 2
- start: float32 [1, 4096, 8192], P(None, 'row', 'col'), may hold values from 0.5 to 2
- psf_rows: float32 [127], replicated, may hold values from 0.05 to 1
- psf_cols: float32 [127], replicated, may hold values from 0.05 to 1
Outputs:
- estimate: float32 [1, 4096, 8192], P(None, 'row', 'col')
- norms: float32 [2], replicated
All inputs are finite; a program needn't handle non-finite values.
Results may differ from a plain program's by a relative error of at most 0.0001.
Values sent between devices are 32-bit elements; how exact they have to be, the bound alone decides.
A program may use at most 64 MiB of HBM per device.

v0:
```python
import jax
import jax.numpy as jnp
from jax import lax
from jax.sharding import PartitionSpec as P

ITERS = 2


def padded_2(block, sides, width):
    for axis, dim in sides:
        count = lax.axis_size(axis)
        forward = [(i, i + 1) for i in range(count - 1)]
        backward = [(target, source) for source, target in forward]
        low = lax.ppermute(
            lax.slice_in_dim(block, block.shape[dim] - width, None, axis=dim), axis, forward
        )
        high = lax.ppermute(lax.slice_in_dim(block, 0, width, axis=dim), axis, backward)
        block = jnp.concatenate([low, block, high], axis=dim)
    return block


def band_matrix(taps, height, width, mirrored):
    ordered = taps[::-1] if mirrored else taps
    diagonal = jnp.concatenate(
        [jnp.zeros((width - 1,), jnp.float32), ordered, jnp.zeros((height - 127,), jnp.float32)]
    )
    period = height + width - 1
    rolled = jnp.concatenate([diagonal[width - 1 :], diagonal[: width - 1]])
    tiled = jnp.tile(rolled, width + 1)[: width * (period - 1)]
    skewed = tiled.reshape(width, period - 1)[:, :height]
    return jnp.transpose(skewed)


def block_width():
    return 128


def tap_table(taps, mirrored):
    block = block_width()
    reach = (block + 126 + block - 1) // block
    return band_matrix(taps, reach * block, block, mirrored)


def blocked_filter(padded, table):
    block = table.shape[1]
    reach = table.shape[0] // block
    length = padded.shape[-1] - 126
    count = length // block
    extra = (count + reach - 1) * block - padded.shape[-1]
    lead = padded.shape[:-1]
    widths = [(0, 0)] * len(lead) + [(0, extra)]
    spread = jnp.pad(padded, widths)
    blocks = spread.reshape(lead + (count + reach - 1, block))
    total = None
    for shift in range(reach):
        term = jnp.einsum(
            "prbj,ji->prbi",
            blocks[..., shift : shift + count, :],
            table[shift * block : (shift + 1) * block],
            precision=lax.Precision.HIGHEST,
        )
        total = term if total is None else total + term
    return total.reshape(lead + (count * block,))


def column_pass(field, table):
    padded = padded_2(field, (("col", 2),), 63)
    return blocked_filter(padded, table)


def row_filter(padded, matrix):
    return jnp.einsum("pjc,ji->pic", padded, matrix, precision=lax.Precision.HIGHEST)


def row_pass(field, matrix):
    padded = padded_2(field, (("row", 1),), 63)
    return row_filter(padded, matrix)


def blur_both(field, col_table, row_matrix):
    return row_pass(column_pass(field, col_table), row_matrix)


def body(observed, start, psf_rows, psf_cols):
    row_taps = psf_rows / jnp.sum(psf_rows)
    col_taps = psf_cols / jnp.sum(psf_cols)
    rows = observed.shape[1]
    blur_cols = tap_table(col_taps, False)
    back_cols = tap_table(col_taps, True)
    blur_rows = band_matrix(row_taps, rows + 126, rows, False)
    back_rows = band_matrix(row_taps, rows + 126, rows, True)
    current = start
    totals = []
    for step in range(ITERS):
        blurred = blur_both(current, blur_cols, blur_rows)
        misfit = observed - blurred
        local_sum = jnp.sum(misfit * misfit)
        totals.append(lax.psum(local_sum, ("row", "col")))
        ratio = observed / blurred
        current = current * blur_both(ratio, back_cols, back_rows)
    norms = jnp.stack(totals)
    return (current, norms)


def solution(mesh):
    in_specs = (P(None, "row", "col"), P(None, "row", "col"), P(), P())
    out_specs = (P(None, "row", "col"), P())
    return jax.shard_map(body, mesh=mesh, in_specs=in_specs, out_specs=out_specs, check_vma=False)
```

profile of v0, /device:TPU:1, one launch (start us, length us, event | category | flops | bytes accessed | tf_op | source)
XLA Modules:
  0.0 205.9 jit_solution(18416084115373391029)
XLA Ops:
  0.6 1.1 copy.12
  1.7 4.8 %collective-permute-start = (f32[1,128,63]{1,2,0:T(8,128)S(1)}, f32[1,128,63]{1,2,0:T(8,128)S(1)}, u32[]{:S(2)}, u32[]{:S(2)}) collective-permute-start(f32[1,128,63]{1,2,0:T(8,128)S(1)} %get-tuple-element.21), channel_id=1, source_target_pairs={{0,1},{1,2},{2,3},{3,4},{4,5},{5,6},{6,7},{7,8},{8,9},{9,10},{10,1... | collective-permute-start | bytes 96776 | tf_op jit(solution)/shard_map/ppermute | solution.py:14
  6.6 1.3 collective-permute-start.1
  8.0 0.6 reduce_sum.37
  8.6 0.6 broadcast_divide_fusion
  9.4 0.3 tile.41
  10.0 0.6 copy-done.3
  10.6 0.6 reduce_sum.36
  11.3 0.6 collective-permute-done.1
  11.9 0.4 fusion.21
  12.3 0.4 convolution_add_fusion.3
  12.8 4.9 %collective-permute-start.2 = (f32[1,63,512]{1,2,0:T(8,128)S(1)}, f32[1,63,512]{1,2,0:T(8,128)S(1)}, u32[]{:S(2)}, u32[]{:S(2)}) collective-permute-start(f32[1,63,512]{1,2,0:T(8,128)S(1)} %get-tuple-element.19), channel_id=1, source_target_pairs={{0,16},{16,32},{32,48},{48,64},{64,80},{80,96},{96,112},{112,128},... | collective-permute-start | bytes 387080 | tf_op jit(solution)/shard_map/ppermute | solution.py:14
  17.8 2.1 %collective-permute-start.3 = (f32[1,63,512]{1,2,0:T(8,128)S(1)}, f32[1,63,512]{1,2,0:T(8,128)S(1)}, u32[]{:S(2)}, u32[]{:S(2)}) collective-permute-start(f32[1,63,512]{1,2,0:T(8,128)S(1)} %get-tuple-element.20), channel_id=1, source_target_pairs={{16,0},{32,16},{48,32},{64,48},{80,64},{96,80},{112,96},{128,112},... | collective-permute-start | bytes 387080 | tf_op jit(solution)/shard_map/ppermute | solution.py:17
  19.9 0.7 broadcast_divide_fusion.2
  21.2 0.3 tile.19
  21.8 3.6 %collective-permute-done.3 = f32[1,63,512]{1,2,0:T(8,128)S(1)} collective-permute-done((f32[1,63,512]{1,2,0:T(8,128)S(1)}, f32[1,63,512]{1,2,0:T(8,128)S(1)}, u32[]{:S(2)}, u32[]{:S(2)}) %collective-permute-start.3) | collective-permute-done | bytes 129056 | tf_op jit(solution)/shard_map/ppermute | solution.py:17
  25.5 0.9 fusion.38
  26.4 4.0 %collective-permute-start.4 = (f32[1,128,63]{2,1,0:T(8,128)S(1)}, f32[1,128,63]{2,1,0:T(8,128)S(1)}, u32[]{:S(2)}, u32[]{:S(2)}) collective-permute-start(f32[1,128,63]{2,1,0:T(8,128)S(1)} %get-tuple-element.17), channel_id=1, source_target_pairs={{0,1},{1,2},{2,3},{3,4},{4,5},{5,6},{6,7},{7,8},{8,9},{9,10},{10,1... | collective-permute-start | bytes 96776 | tf_op jit(solution)/shard_map/ppermute | solution.py:14
  30.4 1.3 collective-permute-start.5
  31.7 5.5 %collective-permute-done.5 = f32[1,128,63]{2,1,0:T(8,128)S(1)} collective-permute-done((f32[1,128,63]{2,1,0:T(8,128)S(1)}, f32[1,128,63]{2,1,0:T(8,128)S(1)}, u32[]{:S(2)}, u32[]{:S(2)}) %collective-permute-start.5) | collective-permute-done | bytes 32288 | tf_op jit(solution)/shard_map/ppermute | solution.py:17
  37.7 0.4 fusion.20
  38.1 0.4 convolution_add_fusion.2
  38.6 2.9 %collective-permute-start.6 = (f32[1,63,512]{1,2,0:T(8,128)S(1)}, f32[1,63,512]{1,2,0:T(8,128)S(1)}, u32[]{:S(2)}, u32[]{:S(2)}) collective-permute-start(f32[1,63,512]{1,2,0:T(8,128)S(1)} %get-tuple-element.15), channel_id=1, source_target_pairs={{0,16},{16,32},{32,48},{48,64},{64,80},{80,96},{96,112},{112,128},... | collective-permute-start | bytes 387080 | tf_op jit(solution)/shard_map/ppermute | solution.py:14
  41.5 1.9 collective-permute-start.7
  43.5 0.3 tile.17
  44.1 0.7 collective-permute-done.6
  44.8 4.4 %collective-permute-done.7 = f32[1,63,512]{1,2,0:T(8,128)S(1)} collective-permute-done((f32[1,63,512]{1,2,0:T(8,128)S(1)}, f32[1,63,512]{1,2,0:T(8,128)S(1)}, u32[]{:S(2)}, u32[]{:S(2)}) %collective-permute-start.7) | collective-permute-done | bytes 129056 | tf_op jit(solution)/shard_map/ppermute | solution.py:17
  49.2 0.9 fusion.1
  50.1 4.8 %collective-permute-start.8 = (f32[1,128,63]{2,1,0:T(8,128)S(1)}, f32[1,128,63]{2,1,0:T(8,128)S(1)}, u32[]{:S(2)}, u32[]{:S(2)}) collective-permute-start(f32[1,128,63]{2,1,0:T(8,128)S(1)} %get-tuple-element.13), channel_id=1, source_target_pairs={{0,1},{1,2},{2,3},{3,4},{4,5},{5,6},{6,7},{7,8},{8,9},{9,10},{10,1... | collective-permute-start | bytes 96776 | tf_op jit(solution)/shard_map/ppermute | solution.py:14
  55.0 1.3 collective-permute-start.9
  56.3 4.1 %collective-permute-done.9 = f32[1,128,63]{2,1,0:T(8,128)S(1)} collective-permute-done((f32[1,128,63]{2,1,0:T(8,128)S(1)}, f32[1,128,63]{2,1,0:T(8,128)S(1)}, u32[]{:S(2)}, u32[]{:S(2)}) %collective-permute-start.9) | collective-permute-done | bytes 32288 | tf_op jit(solution)/shard_map/ppermute | solution.py:17
  60.8 0.4 fusion.19
  61.2 0.4 convolution_add_fusion.1
  61.7 2.9 %collective-permute-start.10 = (f32[1,63,512]{1,2,0:T(8,128)S(1)}, f32[1,63,512]{1,2,0:T(8,128)S(1)}, u32[]{:S(2)}, u32[]{:S(2)}) collective-permute-start(f32[1,63,512]{1,2,0:T(8,128)S(1)} %get-tuple-element.11), channel_id=1, source_target_pairs={{0,16},{16,32},{32,48},{48,64},{64,80},{80,96},{96,112},{112,128},... | collective-permute-start | bytes 387080 | tf_op jit(solution)/shard_map/ppermute | solution.py:14
  64.6 1.9 collective-permute-start.11
  66.6 1.4 collective-permute-done.10
  67.9 4.4 %collective-permute-done.11 = f32[1,63,512]{1,2,0:T(8,128)S(1)} collective-permute-done((f32[1,63,512]{1,2,0:T(8,128)S(1)}, f32[1,63,512]{1,2,0:T(8,128)S(1)}, u32[]{:S(2)}, u32[]{:S(2)}) %collective-permute-start.11) | collective-permute-done | bytes 129056 | tf_op jit(solution)/shard_map/ppermute | solution.py:17
  72.3 1.4 multiply_reduce_fusion.1
  73.8 4.4 %collective-permute-start.12 = (f32[1,128,63]{2,1,0:T(8,128)S(1)}, f32[1,128,63]{2,1,0:T(8,128)S(1)}, u32[]{:S(2)}, u32[]{:S(2)}) collective-permute-start(f32[1,128,63]{2,1,0:T(8,128)S(1)} %get-tuple-element.9), channel_id=1, source_target_pairs={{0,1},{1,2},{2,3},{3,4},{4,5},{5,6},{6,7},{7,8},{8,9},{9,10},{10,1... | collective-permute-start | bytes 96776 | tf_op jit(solution)/shard_map/ppermute | solution.py:14
  78.3 1.3 collective-permute-start.13
  79.6 4.2 %collective-permute-done.13 = f32[1,128,63]{2,1,0:T(8,128)S(1)} collective-permute-done((f32[1,128,63]{2,1,0:T(8,128)S(1)}, f32[1,128,63]{2,1,0:T(8,128)S(1)}, u32[]{:S(2)}, u32[]{:S(2)}) %collective-permute-start.13) | collective-permute-done | bytes 32288 | tf_op jit(solution)/shard_map/ppermute | solution.py:17
  84.1 0.4 fusion.18
  84.5 0.4 convolution_add_fusion
  85.0 3.0 %collective-permute-start.14 = (f32[1,63,512]{1,2,0:T(8,128)S(1)}, f32[1,63,512]{1,2,0:T(8,128)S(1)}, u32[]{:S(2)}, u32[]{:S(2)}) collective-permute-start(f32[1,63,512]{1,2,0:T(8,128)S(1)} %get-tuple-element.7), channel_id=1, source_target_pairs={{0,16},{16,32},{32,48},{48,64},{64,80},{80,96},{96,112},{112,128},... | collective-permute-start | bytes 387080 | tf_op jit(solution)/shard_map/ppermute | solution.py:14
  88.0 1.9 collective-permute-start.15
  89.9 112.5 %all-reduce.6 = (f32[1]{0:T(128)}, f32[1]{0:T(128)}) all-reduce(f32[1]{0:T(128)} %bitcast.31, f32[1]{0:T(128)} %bitcast.30), channel_id=1, replica_groups=mesh['row'=32,'col'=16] {'row','col'}, use_global_device_ids=true, to_apply=%region_5.6 | all-reduce | flops 2 | bytes 16 | tf_op jit(solution)/shard_map/psum | solution.py:98
  202.4 1.9 pad_maximum_fusion.7
  204.3 1.6 fusion
  (52 shorter events, 3.6 us)
Async XLA Ops:
  1.7 6.1 %copy-start.2 = (f32[127]{0:T(128)S(1)}, f32[127]{0:T(128)}, u32[]{:S(2)}) copy-start(f32[127]{0:T(128)} %param.7) | copy-start | bytes 1528
  1.7 9.6 %collective-permute-start = (f32[1,128,63]{1,2,0:T(8,128)S(1)}, f32[1,128,63]{1,2,0:T(8,128)S(1)}, u32[]{:S(2)}, u32[]{:S(2)}) collective-permute-start(f32[1,128,63]{1,2,0:T(8,128)S(1)} %get-tuple-element.21), channel_id=1, source_target_pairs={{0,1},{1,2},{2,3},{3,4},{4,5},{5,6},{6,7},{7,8},{8,9},{9,10},{10,1... | collective-permute-start | bytes 96776 | tf_op jit(solution)/shard_map/ppermute | solution.py:14
  6.6 5.3 %collective-permute-start.1 = (f32[1,128,63]{1,2,0:T(8,128)S(1)}, f32[1,128,63]{1,2,0:T(8,128)S(1)}, u32[]{:S(2)}, u32[]{:S(2)}) collective-permute-start(f32[1,128,63]{1,2,0:T(8,128)S(1)} %get-tuple-element.22), channel_id=1, source_target_pairs={{1,0},{2,1},{3,2},{4,3},{5,4},{6,5},{7,6},{8,7},{9,8},{10,9},{11,1... | collective-permute-start | bytes 96776 | tf_op jit(solution)/shard_map/ppermute | solution.py:17
  9.9 0.7 copy-start.3
  12.8 9.0 %collective-permute-start.2 = (f32[1,63,512]{1,2,0:T(8,128)S(1)}, f32[1,63,512]{1,2,0:T(8,128)S(1)}, u32[]{:S(2)}, u32[]{:S(2)}) collective-permute-start(f32[1,63,512]{1,2,0:T(8,128)S(1)} %get-tuple-element.19), channel_id=1, source_target_pairs={{0,16},{16,32},{32,48},{48,64},{64,80},{80,96},{96,112},{112,128},... | collective-permute-start | bytes 387080 | tf_op jit(solution)/shard_map/ppermute | solution.py:14
  17.8 7.7 %collective-permute-start.3 = (f32[1,63,512]{1,2,0:T(8,128)S(1)}, f32[1,63,512]{1,2,0:T(8,128)S(1)}, u32[]{:S(2)}, u32[]{:S(2)}) collective-permute-start(f32[1,63,512]{1,2,0:T(8,128)S(1)} %get-tuple-element.20), channel_id=1, source_target_pairs={{16,0},{32,16},{48,32},{64,48},{80,64},{96,80},{112,96},{128,112},... | collective-permute-start | bytes 387080 | tf_op jit(solution)/shard_map/ppermute | solution.py:17
  21.6 3.9 %copy-start.1 = (f32[1,128,512]{2,1,0:T(8,128)S(1)}, f32[1,128,512]{2,1,0:T(8,128)}, u32[]{:S(2)}) copy-start(f32[1,128,512]{2,1,0:T(8,128)} %param.4) | copy-start | bytes 786436
  26.4 5.3 %collective-permute-start.4 = (f32[1,128,63]{2,1,0:T(8,128)S(1)}, f32[1,128,63]{2,1,0:T(8,128)S(1)}, u32[]{:S(2)}, u32[]{:S(2)}) collective-permute-start(f32[1,128,63]{2,1,0:T(8,128)S(1)} %get-tuple-element.17), channel_id=1, source_target_pairs={{0,1},{1,2},{2,3},{3,4},{4,5},{5,6},{6,7},{7,8},{8,9},{9,10},{10,1... | collective-permute-start | bytes 96776 | tf_op jit(solution)/shard_map/ppermute | solution.py:14
  30.4 6.9 %collective-permute-start.5 = (f32[1,128,63]{2,1,0:T(8,128)S(1)}, f32[1,128,63]{2,1,0:T(8,128)S(1)}, u32[]{:S(2)}, u32[]{:S(2)}) collective-permute-start(f32[1,128,63]{2,1,0:T(8,128)S(1)} %get-tuple-element.18), channel_id=1, source_target_pairs={{1,0},{2,1},{3,2},{4,3},{5,4},{6,5},{7,6},{8,7},{9,8},{10,9},{11,1... | collective-permute-start | bytes 96776 | tf_op jit(solution)/shard_map/ppermute | solution.py:17
  38.6 6.2 %collective-permute-start.6 = (f32[1,63,512]{1,2,0:T(8,128)S(1)}, f32[1,63,512]{1,2,0:T(8,128)S(1)}, u32[]{:S(2)}, u32[]{:S(2)}) collective-permute-start(f32[1,63,512]{1,2,0:T(8,128)S(1)} %get-tuple-element.15), channel_id=1, source_target_pairs={{0,16},{16,32},{32,48},{48,64},{64,80},{80,96},{96,112},{112,128},... | collective-permute-start | bytes 387080 | tf_op jit(solution)/shard_map/ppermute | solution.py:14
  41.5 7.7 %collective-permute-start.7 = (f32[1,63,512]{1,2,0:T(8,128)S(1)}, f32[1,63,512]{1,2,0:T(8,128)S(1)}, u32[]{:S(2)}, u32[]{:S(2)}) collective-permute-start(f32[1,63,512]{1,2,0:T(8,128)S(1)} %get-tuple-element.16), channel_id=1, source_target_pairs={{16,0},{32,16},{48,32},{64,48},{80,64},{96,80},{112,96},{128,112},... | collective-permute-start | bytes 387080 | tf_op jit(solution)/shard_map/ppermute | solution.py:17
  43.8 5.4 %copy-start = (f32[1,128,512]{2,1,0:T(8,128)S(1)}, f32[1,128,512]{2,1,0:T(8,128)}, u32[]{:S(2)}) copy-start(f32[1,128,512]{2,1,0:T(8,128)} %param.5) | copy-start | bytes 786436
  50.1 6.2 %collective-permute-start.8 = (f32[1,128,63]{2,1,0:T(8,128)S(1)}, f32[1,128,63]{2,1,0:T(8,128)S(1)}, u32[]{:S(2)}, u32[]{:S(2)}) collective-permute-start(f32[1,128,63]{2,1,0:T(8,128)S(1)} %get-tuple-element.13), channel_id=1, source_target_pairs={{0,1},{1,2},{2,3},{3,4},{4,5},{5,6},{6,7},{7,8},{8,9},{9,10},{10,1... | collective-permute-start | bytes 96776 | tf_op jit(solution)/shard_map/ppermute | solution.py:14
  55.0 5.4 %collective-permute-start.9 = (f32[1,128,63]{2,1,0:T(8,128)S(1)}, f32[1,128,63]{2,1,0:T(8,128)S(1)}, u32[]{:S(2)}, u32[]{:S(2)}) collective-permute-start(f32[1,128,63]{2,1,0:T(8,128)S(1)} %get-tuple-element.14), channel_id=1, source_target_pairs={{1,0},{2,1},{3,2},{4,3},{5,4},{6,5},{7,6},{8,7},{9,8},{10,9},{11,1... | collective-permute-start | bytes 96776 | tf_op jit(solution)/shard_map/ppermute | solution.py:17
  61.7 6.2 %collective-permute-start.10 = (f32[1,63,512]{1,2,0:T(8,128)S(1)}, f32[1,63,512]{1,2,0:T(8,128)S(1)}, u32[]{:S(2)}, u32[]{:S(2)}) collective-permute-start(f32[1,63,512]{1,2,0:T(8,128)S(1)} %get-tuple-element.11), channel_id=1, source_target_pairs={{0,16},{16,32},{32,48},{48,64},{64,80},{80,96},{96,112},{112,128},... | collective-permute-start | bytes 387080 | tf_op jit(solution)/shard_map/ppermute | solution.py:14
  64.6 7.7 %collective-permute-start.11 = (f32[1,63,512]{1,2,0:T(8,128)S(1)}, f32[1,63,512]{1,2,0:T(8,128)S(1)}, u32[]{:S(2)}, u32[]{:S(2)}) collective-permute-start(f32[1,63,512]{1,2,0:T(8,128)S(1)} %get-tuple-element.12), channel_id=1, source_target_pairs={{16,0},{32,16},{48,32},{64,48},{80,64},{96,80},{112,96},{128,112},... | collective-permute-start | bytes 387080 | tf_op jit(solution)/shard_map/ppermute | solution.py:17
  73.8 5.7 %collective-permute-start.12 = (f32[1,128,63]{2,1,0:T(8,128)S(1)}, f32[1,128,63]{2,1,0:T(8,128)S(1)}, u32[]{:S(2)}, u32[]{:S(2)}) collective-permute-start(f32[1,128,63]{2,1,0:T(8,128)S(1)} %get-tuple-element.9), channel_id=1, source_target_pairs={{0,1},{1,2},{2,3},{3,4},{4,5},{5,6},{6,7},{7,8},{8,9},{9,10},{10,1... | collective-permute-start | bytes 96776 | tf_op jit(solution)/shard_map/ppermute | solution.py:14
  78.3 5.5 %collective-permute-start.13 = (f32[1,128,63]{2,1,0:T(8,128)S(1)}, f32[1,128,63]{2,1,0:T(8,128)S(1)}, u32[]{:S(2)}, u32[]{:S(2)}) collective-permute-start(f32[1,128,63]{2,1,0:T(8,128)S(1)} %get-tuple-element.10), channel_id=1, source_target_pairs={{1,0},{2,1},{3,2},{4,3},{5,4},{6,5},{7,6},{8,7},{9,8},{10,9},{11,1... | collective-permute-start | bytes 96776 | tf_op jit(solution)/shard_map/ppermute | solution.py:17
  85.0 119.3 %collective-permute-start.14 = (f32[1,63,512]{1,2,0:T(8,128)S(1)}, f32[1,63,512]{1,2,0:T(8,128)S(1)}, u32[]{:S(2)}, u32[]{:S(2)}) collective-permute-start(f32[1,63,512]{1,2,0:T(8,128)S(1)} %get-tuple-element.7), channel_id=1, source_target_pairs={{0,16},{16,32},{32,48},{48,64},{64,80},{80,96},{96,112},{112,128},... | collective-permute-start | bytes 387080 | tf_op jit(solution)/shard_map/ppermute | solution.py:14
  88.0 116.3 %collective-permute-start.15 = (f32[1,63,512]{1,2,0:T(8,128)S(1)}, f32[1,63,512]{1,2,0:T(8,128)S(1)}, u32[]{:S(2)}, u32[]{:S(2)}) collective-permute-start(f32[1,63,512]{1,2,0:T(8,128)S(1)} %get-tuple-element.8), channel_id=1, source_target_pairs={{16,0},{32,16},{48,32},{64,48},{80,64},{96,80},{112,96},{128,112},... | collective-permute-start | bytes 387080 | tf_op jit(solution)/shard_map/ppermute | solution.py:17
where the time goes:
time: 207 us; the launch traced here: 206 us
  blocking collectives  112 us (54%)
  starting transfers between devices  44.8 us (22%)
  waiting for transfers between devices  28.9 us (14%)
  matrix products  7.85 us (4%)
  local copies, waits for them, and re-layouts  5.61 us (3%)
  other arithmetic  5.04 us (2%)
    psum x1, blocking collectives, body(): totals.append(lax.psum(local_sum, ('row', 'col')))  112 us
    ppermute x8, starting transfers between devices, padded_2(): lax.ppermute(lax.slice_in_dim(block, block.shape[dim] - width, None, axis...  31.7 us
    ppermute x8, waiting for transfers between devices, padded_2(): lax.ppermute(lax.slice_in_dim(block, 0, width, axis=dim), axis, backward)  26.8 us
    ppermute x8, starting transfers between devices, padded_2(): lax.ppermute(lax.slice_in_dim(block, 0, width, axis=dim), axis, backward)  13.1 us
    dot_general x4, matrix products, row_filter(): jnp.einsum('pjc,ji->pic', padded, matrix, precision=lax.Precision.HIGHEST)  4.71 us
  transfers between devices with their start and end apart: 16, of which 9 were waited for; matrix products, arithmetic and copies ran while one was open for 3% of the time, Pallas kernels for 0%

commit v1 on v0

v1 whole, which is shorter than its diff:
```python
import functools

import jax
import jax.numpy as jnp
from jax import lax
from jax.experimental import pallas as pl
from jax.experimental.pallas import tpu as pltpu
from jax.sharding import PartitionSpec as P

ITERS = 2
STAGES = 2 * ITERS
MESH = pl.DeviceIdType.MESH
STEPS = ((-1, -1), (-1, 1), (1, -1), (1, 1), (0, -1), (0, 1), (-1, 0), (1, 0))


def split(value):
    high = value.astype(jnp.bfloat16)
    low = (value - high.astype(jnp.float32)).astype(jnp.bfloat16)
    return high, low


def dot(left, right):
    return jnp.dot(left, right, preferred_element_type=jnp.float32)


def circulant(taps, shift, rows):
    wide = jnp.broadcast_to(taps, (rows, 256))
    return pltpu.roll(wide, shift % 256, 1, stride=1, stride_axis=0)


def kernel(
    rows, cols, obs_hbm, start_hbm, taps_rows, taps_cols, out_ref, norms_ref,
    field, left, right, pack_left, pack_right, seen, current, result, taps,
    row_mats, col_mats, partial, gather_rows, middle, gather_cols,
    send, recv, local, norm_send, norm_recv,
):
    row, col = lax.axis_index("row"), lax.axis_index("col")

    load_start = pltpu.make_async_copy(start_hbm, field.at[0, pl.ds(64, 128)], local.at[0])
    load_seen = pltpu.make_async_copy(obs_hbm, seen, local.at[1])
    load_start.start()
    load_seen.start()

    def near(step):
        r, c = row + step[0], col + step[1]
        inside = (r >= 0) & (r < rows) & (c >= 0) & (c < cols)
        return inside, (r, c)

    barrier = pltpu.get_barrier_semaphore()
    expected = jnp.int32(rows - 1 + cols - 1)
    for step in STEPS[:4]:
        inside, device = near(step)

        @pl.when(inside)
        def _():
            pl.semaphore_signal(barrier, inc=1, device_id=device, device_id_type=MESH)

        expected = expected + inside.astype(jnp.int32)

    def greet_row(d, carry):
        pl.semaphore_signal(
            barrier, inc=1, device_id=(lax.rem(row + d, rows), col), device_id_type=MESH
        )
        return carry

    def greet_col(d, carry):
        pl.semaphore_signal(
            barrier, inc=1, device_id=(row, lax.rem(col + d, cols)), device_id_type=MESH
        )
        return carry

    lax.fori_loop(1, rows, greet_row, 0)
    lax.fori_loop(1, cols, greet_col, 0)

    @pl.when(row == 0)
    def _():
        field[:, 0:64, :] = jnp.zeros((STAGES, 64, 512), jnp.float32)
        left[:, 0:32, :] = jnp.zeros((STAGES, 32, 128), jnp.float32)
        right[:, 0:32, :] = jnp.zeros((STAGES, 32, 128), jnp.float32)

    @pl.when(row == rows - 1)
    def _():
        field[:, 192:256, :] = jnp.zeros((STAGES, 64, 512), jnp.float32)
        left[:, 96:128, :] = jnp.zeros((STAGES, 32, 128), jnp.float32)
        right[:, 96:128, :] = jnp.zeros((STAGES, 32, 128), jnp.float32)

    @pl.when(col == 0)
    def _():
        left[...] = jnp.zeros((STAGES, 128, 128), jnp.float32)

    @pl.when(col == cols - 1)
    def _():
        right[...] = jnp.zeros((STAGES, 128, 128), jnp.float32)

    taps[...] = jnp.zeros((8, 256), jnp.float32)
    taps[0:1, 0:127] = taps_rows[...] / jnp.sum(taps_rows[...])
    taps[1:2, 0:127] = taps_cols[...] / jnp.sum(taps_cols[...])
    row_taps, col_taps = taps[0:1, :], taps[1:2, :]
    by_rows = (circulant(row_taps, 1, 128), circulant(row_taps, -127, 256)[:, :128].T)
    along = circulant(col_taps, -63, 256)
    by_cols = (along[:128].T, along[:, :128])
    for which in range(2):
        high, low = split(by_rows[which])
        row_mats[which, 0:128, :] = high
        row_mats[which, 128:256, :] = low
        high, low = split(by_cols[which])
        col_mats[which, :, 0:128] = high
        col_mats[which, :, 128:256] = low

    lane = lax.broadcasted_iota(jnp.int32, (32, 128), 1) < 64
    lane_tall = lax.broadcasted_iota(jnp.int32, (128, 128), 1) < 64

    def copies(stage):
        own = field.at[stage]
        ends = {
            (-1, 0): (own.at[pl.ds(64, 64)], own.at[pl.ds(192, 64)]),
            (1, 0): (own.at[pl.ds(128, 64)], own.at[pl.ds(0, 64)]),
            (0, -1): (pack_left.at[stage], right.at[stage, pl.ds(32, 64)]),
            (0, 1): (pack_right.at[stage], left.at[stage, pl.ds(32, 64)]),
            (-1, -1): (pack_left.at[stage, pl.ds(0, 32)], right.at[stage, pl.ds(96, 32)]),
            (-1, 1): (pack_right.at[stage, pl.ds(0, 32)], left.at[stage, pl.ds(96, 32)]),
            (1, -1): (pack_left.at[stage, pl.ds(32, 32)], right.at[stage, pl.ds(0, 32)]),
            (1, 1): (pack_right.at[stage, pl.ds(32, 32)], left.at[stage, pl.ds(0, 32)]),
        }
        made = []
        for k, step in enumerate(STEPS):
            inside, device = near(step)
            source, target = ends[step]
            copy = pltpu.make_async_remote_copy(
                src_ref=source,
                dst_ref=target,
                send_sem=send.at[stage, k],
                recv_sem=recv.at[stage, k],
                device_id=device,
                device_id_type=MESH,
            )
            made.append((step, inside, copy))
        return made

    def post(stage):
        for half in range(2):
            at = 64 + 64 * half
            first = field[stage, at : at + 32, 0:128]
            second = field[stage, at + 32 : at + 64, 0:128]
            pack_left[stage, 32 * half : 32 * half + 32, :] = jnp.where(
                lane, first, pltpu.roll(second, 64, 1)
            )
            first = field[stage, at : at + 32, 384:512]
            second = field[stage, at + 32 : at + 64, 384:512]
            pack_right[stage, 32 * half : 32 * half + 32, :] = jnp.where(
                lane, pltpu.roll(second, 64, 1), first
            )
        for _, inside, copy in copies(stage):

            @pl.when(inside)
            def _():
                copy.start()

    def arrive(stage):
        for step, _, copy in copies(stage):
            inside, _ = near((-step[0], -step[1]))

            @pl.when(inside)
            def _():
                copy.wait_recv()

    def depart(stage):
        for _, inside, copy in copies(stage):

            @pl.when(inside)
            def _():
                copy.wait_send()

    def blur(stage, which):
        sides = []
        for group in range(4):
            from_left = left[stage, 32 * group : 32 * group + 32, :]
            from_right = right[stage, 32 * group : 32 * group + 32, :]
            sides.append(jnp.where(lane, from_right, from_left))
            sides.append(pltpu.roll(jnp.where(lane, from_left, from_right), 64, 1))
        wide = jnp.concatenate([field[stage], jnp.concatenate(sides, axis=0)], axis=1)
        high, low = split(wide)
        both = dot(row_mats[which], high)
        tall = both[0:128] + both[128:256] + dot(row_mats[which, 0:128, :], low)
        blocks = [tall[:, 128 * b : 128 * b + 128] for b in range(5)]
        pairs = []
        for b in range(4):
            mixed = jnp.where(lane_tall, blocks[b + 1], blocks[b - 1])
            pairs.append(jnp.concatenate([blocks[b], mixed], axis=1))
        high, low = split(jnp.concatenate(pairs, axis=0))
        both = dot(high, col_mats[which])
        flat = both[:, 0:128] + both[:, 128:256] + dot(low, col_mats[which, :, 0:128])
        return [flat[128 * b : 128 * b + 128] for b in range(4)]

    def norm_row(d):
        to = lax.rem(row + d, rows)
        return pltpu.make_async_remote_copy(
            src_ref=partial,
            dst_ref=gather_rows.at[row],
            send_sem=norm_send.at[0],
            recv_sem=norm_recv.at[0],
            device_id=(to, col),
            device_id_type=MESH,
        )

    def norm_col(d):
        to = lax.rem(col + d, cols)
        return pltpu.make_async_remote_copy(
            src_ref=middle,
            dst_ref=gather_cols.at[col],
            send_sem=norm_send.at[1],
            recv_sem=norm_recv.at[1],
            device_id=(row, to),
            device_id_type=MESH,
        )

    def wait_all(buffer, count, index, which):
        whole = buffer.at[pl.ds(0, count)]
        copy = pltpu.make_async_copy(whole, whole, which.at[index])
        copy.wait()

    def start_norm_row(d, carry):
        norm_row(d).start()
        return carry

    def start_norm_col(d, carry):
        norm_col(d).start()
        return carry

    load_start.wait()
    pl.semaphore_wait(barrier, expected)

    for stage in range(STAGES):
        post(stage)
        if stage == 0:
            current[...] = field[0, 64:192, :]
            load_seen.wait()
        arrive(stage)
        outs = blur(stage, stage % 2)
        if stage % 2 == 0:
            total = jnp.zeros((1, 128), jnp.float32)
            for b in range(4):
                misfit = seen[:, 128 * b : 128 * b + 128] - outs[b]
                total = total + jnp.sum(misfit * misfit, axis=0, keepdims=True)
            partial[stage // 2 : stage // 2 + 1, :] = total
            if stage == STAGES - 2:
                gather_rows[row] = partial[...]
                lax.fori_loop(1, rows, start_norm_row, 0)
            for b in range(4):
                field[stage + 1, 64:192, 128 * b : 128 * b + 128] = (
                    seen[:, 128 * b : 128 * b + 128] / outs[b]
                )
        else:
            target = field.at[stage + 1, pl.ds(64, 128)] if stage + 1 < STAGES else result
            for b in range(4):
                value = current[:, 128 * b : 128 * b + 128] * outs[b]
                target[:, 128 * b : 128 * b + 128] = value
                if stage + 1 < STAGES:
                    current[:, 128 * b : 128 * b + 128] = value

    store = pltpu.make_async_copy(result, out_ref, local.at[2])
    store.start()
    wait_all(gather_rows, rows - 1, 0, norm_recv)
    total = gather_rows[0]
    for r in range(1, rows):
        total = total + gather_rows[r]
    middle[...] = total
    gather_cols[col] = total
    lax.fori_loop(1, cols, start_norm_col, 0)
    for stage in range(STAGES):
        depart(stage)
    wait_all(gather_rows, rows - 1, 0, norm_send)
    wait_all(gather_cols, cols - 1, 1, norm_recv)
    total = gather_cols[0]
    for c in range(1, cols):
        total = total + gather_cols[c]
    sums = jnp.sum(total, axis=1, keepdims=True)
    place = lax.broadcasted_iota(jnp.int32, (1, 2), 1)
    norms_ref[...] = jnp.where(place == 0, sums[0:1], sums[1:2])
    wait_all(gather_cols, cols - 1, 1, norm_send)
    store.wait()


def body(rows, cols, observed, start, psf_rows, psf_cols):
    f32, bf16 = jnp.float32, jnp.bfloat16
    estimate, norms = pl.pallas_call(
        functools.partial(kernel, rows, cols),
        out_shape=(
            jax.ShapeDtypeStruct((128, 512), f32),
            jax.ShapeDtypeStruct((1, 2), f32),
        ),
        in_specs=[
            pl.BlockSpec(memory_space=pl.ANY),
            pl.BlockSpec(memory_space=pl.ANY),
            pl.BlockSpec(memory_space=pltpu.VMEM),
            pl.BlockSpec(memory_space=pltpu.VMEM),
        ],
        out_specs=(
            pl.BlockSpec(memory_space=pl.ANY),
            pl.BlockSpec(memory_space=pltpu.VMEM),
        ),
        scratch_shapes=[
            pltpu.VMEM((STAGES, 256, 512), f32),
            pltpu.VMEM((STAGES, 128, 128), f32),
            pltpu.VMEM((STAGES, 128, 128), f32),
            pltpu.VMEM((STAGES, 64, 128), f32),
            pltpu.VMEM((STAGES, 64, 128), f32),
            pltpu.VMEM((128, 512), f32),
            pltpu.VMEM((128, 512), f32),
            pltpu.VMEM((128, 512), f32),
            pltpu.VMEM((8, 256), f32),
            pltpu.VMEM((2, 256, 256), bf16),
            pltpu.VMEM((2, 256, 256), bf16),
            pltpu.VMEM((2, 128), f32),
            pltpu.VMEM((rows, 2, 128), f32),
            pltpu.VMEM((2, 128), f32),
            pltpu.VMEM((cols, 2, 128), f32),
            pltpu.SemaphoreType.DMA((STAGES, 8)),
            pltpu.SemaphoreType.DMA((STAGES, 8)),
            pltpu.SemaphoreType.DMA((3,)),
            pltpu.SemaphoreType.DMA((2,)),
            pltpu.SemaphoreType.DMA((2,)),
        ],
        compiler_params=pltpu.CompilerParams(
            collective_id=0, has_side_effects=True, vmem_limit_bytes=48 * 1024 * 1024
        ),
        name="deconvolve",
    )(observed[0], start[0], psf_rows.reshape(1, 127), psf_cols.reshape(1, 127))
    return estimate[None], norms.reshape(2)


def solution(mesh):
    in_specs = (P(None, "row", "col"), P(None, "row", "col"), P(), P())
    out_specs = (P(None, "row", "col"), P())
    step = functools.partial(body, mesh.shape["row"], mesh.shape["col"])
    return jax.shard_map(step, mesh=mesh, in_specs=in_specs, out_specs=out_specs, check_vma=False)
```

time: 207 us -> 48.9 us (0.24)
  blocking collectives: 112 us -> 0 us
  starting transfers between devices: 44.8 us -> 0 us
  Pallas kernels: 0 us -> 43.8 us
  waiting for transfers between devices: 28.9 us -> 0 us
  matrix products: 7.85 us -> 0 us
  other arithmetic: 5.04 us -> 0 us
    psum x1 -> x0, blocking collectives: 112 us -> none  [body(): totals.append(lax.psum(local_sum, ('row', 'col')))]
    ppermute x16 -> x0, starting transfers between devices: 44.8 us -> none  [the longest x8 31.7 us: padded_2(): lax.ppermute(lax.slice_in_dim(block, block.shape[dim] - width, None, axis...]
    pallas_call x0 -> x1, Pallas kernels: none -> 43.8 us  [body(): pl.pallas_call(functools.partial(kernel, rows, cols), out_shape=(jax.Shap...]
    ppermute x16 -> x0, waiting for transfers between devices: 28.9 us -> none  [the longest x8 26.8 us: padded_2(): lax.ppermute(lax.slice_in_dim(block, 0, width, axis=dim), axis, backward)]
    dot_general x12 -> x0, matrix products: 7.85 us -> none  [the longest x4 4.71 us: row_filter(): jnp.einsum('pjc,ji->pic', padded, matrix, precision=lax.Precision.HIGHEST)]
  transfers between devices with their start and end apart: 16 -> 0, of which waited for: 9 -> 0; matrix products, arithmetic and copies ran while one was open for 3% -> 0% of each run, Pallas kernels for 0% -> 0%
where the time goes in v1:
time: 48.9 us; the launch traced here: 48.3 us
  Pallas kernels  43.8 us (90%)
  local copies, waits for them, and re-layouts  3.77 us (8%)
  between operations  0.66 us (1%)
    pallas_call x1, Pallas kernels, body(): pl.pallas_call(functools.partial(kernel, rows, cols), out_shape=(jax.Shap...  43.8 us
    unnamed x10, local copies, waits for them, and re-layouts  3.77 us

profile of v1, /device:TPU:1, one launch (start us, length us, event | category | flops | bytes accessed | tf_op | source)
XLA Modules:
  0.0 48.3 jit_solution(4944989011875855601)
XLA Ops:
  0.6 0.0 copy-start.2
  0.6 0.0 copy-start.3
  0.7 0.6 %copy-done.2 = f32[127]{0:T(128)S(1)} copy-done((f32[127]{0:T(128)S(1)}, f32[127]{0:T(128)}, u32[]{:S(2)}) %copy-start.2) | copy-done | bytes 532
  1.3 0.0 copy-done.3
  1.3 0.0 copy-start
  1.3 0.9 %copy-done = f32[1,128,512]{2,1,0:T(8,128)S(1)} copy-done((f32[1,128,512]{2,1,0:T(8,128)S(1)}, f32[1,128,512]{2,1,0:T(8,128)}, u32[]{:S(2)}) %copy-start) | copy-done | bytes 262168
  2.3 0.0 copy-start.1
  2.3 0.9 %copy-done.1 = f32[1,128,512]{2,1,0:T(8,128)S(1)} copy-done((f32[1,128,512]{2,1,0:T(8,128)S(1)}, f32[1,128,512]{2,1,0:T(8,128)}, u32[]{:S(2)}) %copy-start.1) | copy-done | bytes 262168
  3.2 43.8 %deconvolve.1 = (f32[128,512]{1,0:T(8,128)S(1)}, f32[1,2]{1,0:T(1,128)S(1)}) custom-call(f32[128,512]{1,0:T(8,128)S(1)} %bitcast.6, f32[128,512]{1,0:T(8,128)S(1)} %bitcast.7, f32[1,127]{1,0:T(1,128)S(1)} %bitcast.9, f32[1,127]{1,0:T(1,128)S(1)} %bitcast.10), custom_call_target="tpu_custom_call" | custom-call | tf_op jit(solution)/shard_map/deconvolve/pallas_call | solution.py:286
  47.0 0.7 %copy.8 = f32[1,128,512]{2,1,0:T(8,128)} copy(f32[1,128,512]{2,1,0:T(8,128)S(1)} %bitcast.8) | data formatting | bytes 524288
  47.7 0.5 %copy.9 = f32[2]{0:T(128)} copy(f32[2]{0:T(128)S(1)} %bitcast.11) | data formatting | bytes 16
Async XLA Ops:
  0.6 0.7 %copy-start.2 = (f32[127]{0:T(128)S(1)}, f32[127]{0:T(128)}, u32[]{:S(2)}) copy-start(f32[127]{0:T(128)} %param.6) | copy-start | bytes 1528
  0.6 0.7 %copy-start.3 = (f32[127]{0:T(128)S(1)}, f32[127]{0:T(128)}, u32[]{:S(2)}) copy-start(f32[127]{0:T(128)} %param.7) | copy-start | bytes 1528
  1.3 0.9 %copy-start = (f32[1,128,512]{2,1,0:T(8,128)S(1)}, f32[1,128,512]{2,1,0:T(8,128)}, u32[]{:S(2)}) copy-start(f32[1,128,512]{2,1,0:T(8,128)} %param.4) | copy-start | bytes 786436
  2.3 0.9 %copy-start.1 = (f32[1,128,512]{2,1,0:T(8,128)S(1)}, f32[1,128,512]{2,1,0:T(8,128)}, u32[]{:S(2)}) copy-start(f32[1,128,512]{2,1,0:T(8,128)} %param.5) | copy-start | bytes 786436

commit v2 on v1

v2 whole, which is shorter than its diff:
```python
import functools

import jax
import jax.numpy as jnp
from jax import lax
from jax.experimental import pallas as pl
from jax.experimental.pallas import tpu as pltpu
from jax.sharding import PartitionSpec as P

ITERS = 2
STAGES = 2 * ITERS
MESH = pl.DeviceIdType.MESH
SIDES = ((-1, -1), (-1, 1), (1, -1), (1, 1), (0, -1), (0, 1))
ENDS = ((-1, 0), (1, 0))


def split(value):
    high = value.astype(jnp.bfloat16)
    low = (value - high.astype(jnp.float32)).astype(jnp.bfloat16)
    return high, low


def dot(left, right):
    return jnp.dot(left, right, preferred_element_type=jnp.float32)


def circulant(taps, shift, rows):
    wide = jnp.broadcast_to(taps, (rows, 256))
    return pltpu.roll(wide, shift % 256, 1, stride=1, stride_axis=0)


def doublings(count):
    return max(count - 2, 0).bit_length()


def kernel(
    rows, cols, obs_hbm, start_hbm, rows_hbm, cols_hbm, out_ref, norms_ref,
    field, left, right, pack_left, pack_right, seen, result, taps_rows, taps_cols, taps,
    row_mats, col_mats, partial, gather_rows, middle, gather_cols,
    send_sides, recv_sides, send_rows, recv_rows, local, norm_send, norm_recv, known,
):
    row, col = lax.axis_index("row"), lax.axis_index("col")

    load_start = pltpu.make_async_copy(start_hbm, field.at[0, pl.ds(64, 128)], local.at[0])
    load_seen = pltpu.make_async_copy(obs_hbm, seen, local.at[1])
    load_rows = pltpu.make_async_copy(rows_hbm, taps_rows, local.at[2])
    load_cols = pltpu.make_async_copy(cols_hbm, taps_cols, local.at[3])
    load_start.start()

    def near(step):
        r, c = row + step[0], col + step[1]
        inside = (r >= 0) & (r < rows) & (c >= 0) & (c < cols)
        return inside, (r, c)

    barrier = pltpu.get_barrier_semaphore()
    expected = jnp.int32(0)
    for step in SIDES + ENDS:
        inside, device = near(step)

        @pl.when(inside)
        def _():
            pl.semaphore_signal(barrier, inc=1, device_id=device, device_id_type=MESH)

        expected = expected + inside.astype(jnp.int32)

    load_seen.start()
    load_rows.start()
    load_cols.start()

    lane = lax.broadcasted_iota(jnp.int32, (32, 128), 1) < 64
    lane_tall = lax.broadcasted_iota(jnp.int32, (128, 128), 1) < 64

    def remote(step, source, target, sent, received):
        inside, device = near(step)
        copy = pltpu.make_async_remote_copy(
            src_ref=source,
            dst_ref=target,
            send_sem=sent,
            recv_sem=received,
            device_id=device,
            device_id_type=MESH,
        )
        return step, inside, copy

    def side_copies(stage):
        ends = {
            (0, -1): (pack_left.at[stage], right.at[stage, pl.ds(32, 64)]),
            (0, 1): (pack_right.at[stage], left.at[stage, pl.ds(32, 64)]),
            (-1, -1): (pack_left.at[stage, pl.ds(0, 32)], right.at[stage, pl.ds(96, 32)]),
            (-1, 1): (pack_right.at[stage, pl.ds(0, 32)], left.at[stage, pl.ds(96, 32)]),
            (1, -1): (pack_left.at[stage, pl.ds(32, 32)], right.at[stage, pl.ds(0, 32)]),
            (1, 1): (pack_right.at[stage, pl.ds(32, 32)], left.at[stage, pl.ds(0, 32)]),
        }
        return [
            remote(step, *ends[step], send_sides.at[stage, k], recv_sides.at[stage, k])
            for k, step in enumerate(SIDES)
        ]

    def row_copies(stage, blocks):
        made = []
        for k, step in enumerate(ENDS):
            source, target = ((64, 192), (128, 0))[k]
            for b in blocks:
                lanes = pl.ds(128 * b, 128)
                made.append(
                    remote(
                        step,
                        field.at[stage, pl.ds(source, 64), lanes],
                        field.at[stage, pl.ds(target, 64), lanes],
                        send_rows.at[stage, k, b],
                        recv_rows.at[stage, k, b],
                    )
                )
        return made

    def start(copies):
        for _, inside, copy in copies:

            @pl.when(inside)
            def _():
                copy.start()

    def arrive(copies):
        for step, _, copy in copies:
            inside, _ = near((-step[0], -step[1]))

            @pl.when(inside)
            def _():
                copy.wait_recv()

    def depart(copies):
        for _, inside, copy in copies:

            @pl.when(inside)
            def _():
                copy.wait_send()

    def pack(stage, edge):
        for half in range(2):
            first = edge[64 * half : 64 * half + 32]
            second = pltpu.roll(edge[64 * half + 32 : 64 * half + 64], 64, 1)
            rows_here = slice(32 * half, 32 * half + 32)
            pack_left[stage, rows_here, :] = jnp.where(lane, first, second)
            pack_right[stage, rows_here, :] = jnp.where(lane, second, first)

    def along_rows(which, value):
        high, low = split(value)
        both = dot(row_mats[which], high)
        return both[0:128] + both[128:256] + dot(row_mats[which, 0:128, :], low)

    def along_cols(which, blocks, first, second):
        nothing = jnp.zeros((128, 128), jnp.float32)
        pairs = []
        for b in (first, second):
            mixed = jnp.where(lane_tall, blocks.get(b + 1, nothing), blocks.get(b - 1, nothing))
            pairs.append(jnp.concatenate([blocks[b], mixed], axis=1))
        high, low = split(jnp.concatenate(pairs, axis=0))
        both = dot(high, col_mats[which])
        flat = both[:, 0:128] + both[:, 128:256] + dot(low, col_mats[which, :, 0:128])
        return flat[0:128], flat[128:256]

    def along_cols_edge(which, halo):
        high, low = split(halo)
        both = dot(high, col_mats[which, 128:256, :])
        return both[:, 0:128] + both[:, 128:256] + dot(low, col_mats[which, 128:256, 0:128])

    def sides(stage):
        parts = []
        for group in range(4):
            from_left = left[stage, 32 * group : 32 * group + 32, :]
            from_right = right[stage, 32 * group : 32 * group + 32, :]
            parts.append(jnp.where(lane, from_right, from_left))
            parts.append(pltpu.roll(jnp.where(lane, from_left, from_right), 64, 1))
        return jnp.concatenate(parts, axis=0)

    def squares(difference):
        return jnp.sum(difference * difference, axis=0, keepdims=True)

    def norm_row(d):
        return pltpu.make_async_remote_copy(
            src_ref=partial,
            dst_ref=gather_rows.at[row],
            send_sem=norm_send.at[0],
            recv_sem=norm_recv.at[0],
            device_id=(lax.rem(row + d, rows), col),
            device_id_type=MESH,
        )

    def norm_col(d):
        return pltpu.make_async_remote_copy(
            src_ref=middle,
            dst_ref=gather_cols.at[col],
            send_sem=norm_send.at[1],
            recv_sem=norm_recv.at[1],
            device_id=(row, lax.rem(col + d, cols)),
            device_id_type=MESH,
        )

    def wait_all(buffer, count, semaphore):
        whole = buffer.at[pl.ds(0, count)]
        pltpu.make_async_copy(whole, whole, semaphore).wait()

    def start_norm_row(d, carry):
        norm_row(d).start()
        return carry

    def start_norm_col(d, carry):
        norm_col(d).start()
        return carry

    def tell(level):
        for k, steps in enumerate(((1, 0), (0, 1))):
            if 1 << level < (rows, cols)[k] - 1:
                for sign in (-1, 1):
                    inside, device = near(tuple(sign * (1 << level) * s for s in steps))

                    @pl.when(inside)
                    def _():
                        pl.semaphore_signal(
                            known.at[level, k], inc=1, device_id=device, device_id_type=MESH
                        )

    def hear(level):
        for k, steps in enumerate(((1, 0), (0, 1))):
            if 1 << level < (rows, cols)[k] - 1:
                told = jnp.int32(0)
                for sign in (-1, 1):
                    inside, _ = near(tuple(sign * (1 << level) * s for s in steps))
                    told = told + inside.astype(jnp.int32)
                pl.semaphore_wait(known.at[level, k], told)

    load_start.wait()
    pack(0, jnp.where(lane_tall, field[0, 64:192, 0:128], field[0, 64:192, 384:512]))
    pl.semaphore_wait(barrier, expected)
    start(side_copies(0))
    start(row_copies(0, (0, 1, 2, 3)))
    tell(0)

    @pl.when(row == 0)
    def _():
        field[:, 0:64, :] = jnp.zeros((STAGES, 64, 512), jnp.float32)
        left[:, 0:32, :] = jnp.zeros((STAGES, 32, 128), jnp.float32)
        right[:, 0:32, :] = jnp.zeros((STAGES, 32, 128), jnp.float32)

    @pl.when(row == rows - 1)
    def _():
        field[:, 192:256, :] = jnp.zeros((STAGES, 64, 512), jnp.float32)
        left[:, 96:128, :] = jnp.zeros((STAGES, 32, 128), jnp.float32)
        right[:, 96:128, :] = jnp.zeros((STAGES, 32, 128), jnp.float32)

    @pl.when(col == 0)
    def _():
        left[...] = jnp.zeros((STAGES, 128, 128), jnp.float32)

    @pl.when(col == cols - 1)
    def _():
        right[...] = jnp.zeros((STAGES, 128, 128), jnp.float32)

    load_rows.wait()
    load_cols.wait()
    taps[...] = jnp.zeros((8, 256), jnp.float32)
    taps[0:1, 0:127] = taps_rows[...] / jnp.sum(taps_rows[...])
    taps[1:2, 0:127] = taps_cols[...] / jnp.sum(taps_cols[...])
    row_taps, col_taps = taps[0:1, :], taps[1:2, :]
    by_rows = (circulant(row_taps, 1, 128), circulant(row_taps, -127, 256)[:, :128].T)
    along = circulant(col_taps, -63, 256)
    by_cols = (along[:128].T, along[:, :128])
    for which in range(2):
        high, low = split(by_rows[which])
        row_mats[which, 0:128, :] = high
        row_mats[which, 128:256, :] = low
        high, low = split(by_cols[which])
        col_mats[which, :, 0:128] = high
        col_mats[which, :, 128:256] = low
    load_seen.wait()

    def updated(stage, own, blurred):
        return own / blurred if stage % 2 == 0 else own * blurred

    levels = max(doublings(rows), doublings(cols))
    hear(0)
    tell(1)
    heard = 1
    for stage in range(STAGES):
        which, last = stage % 2, stage + 1 == STAGES
        if last:
            wait_all(gather_rows, rows - 1, norm_recv.at[0])
            total = gather_rows[0]
            for r in range(1, rows):
                total = total + gather_rows[r]
            middle[...] = total
            gather_cols[col] = total
            lax.fori_loop(1, cols, start_norm_col, 0)

        def own(b):
            lanes = slice(128 * b, 128 * b + 128)
            return seen[:, lanes] if which == 0 else field[stage - 1, 64:192, lanes]

        def put(b, value):
            lanes = slice(128 * b, 128 * b + 128)
            if last:
                result[:, lanes] = value
            else:
                field[stage + 1, 64:192, lanes] = value

        blocks, outs = {}, {}
        arrive(row_copies(stage, (1, 2)))
        both = along_rows(which, field[stage, :, 128:384])
        blocks[1], blocks[2] = both[:, 0:128], both[:, 128:256]
        arrive(row_copies(stage, (0, 3)))
        both = along_rows(
            which, jnp.concatenate([field[stage, :, 0:128], field[stage, :, 384:512]], axis=1)
        )
        blocks[0], blocks[3] = both[:, 0:128], both[:, 128:256]
        outs[1], outs[2] = along_cols(which, blocks, 1, 2)
        for b in (1, 2):
            put(b, updated(stage, own(b), outs[b]))
        if not last:
            start(row_copies(stage + 1, (1, 2)))
        outs[0], outs[3] = along_cols(which, blocks, 0, 3)
        inner = {b: updated(stage, own(b), outs[b]) for b in (0, 3)}
        if which == 0:
            partial_sum = squares(own(1) - outs[1]) + squares(own(2) - outs[2])
            partial_sum = partial_sum + squares(
                jnp.where(lane_tall, own(3) - outs[3], own(0) - outs[0])
            )
        own_edge = jnp.where(lane_tall, own(0), own(3))
        edge = jnp.where(lane_tall, outs[0], outs[3])
        if stage > 0 and heard < levels:
            hear(heard)
            heard += 1
            tell(heard)
        arrive(side_copies(stage))
        edge = edge + along_cols_edge(which, along_rows(which, sides(stage)))
        if stage == STAGES - 2:
            partial[ITERS - 1 : ITERS, :] = partial_sum + squares(own_edge - edge)
            gather_rows[row] = partial[...]
            lax.fori_loop(1, rows, start_norm_row, 0)
        outer = updated(stage, own_edge, edge)
        if not last:
            pack(stage + 1, outer)
            start(side_copies(stage + 1))
        put(0, jnp.where(lane_tall, outer, inner[0]))
        put(3, jnp.where(lane_tall, inner[3], outer))
        if not last:
            start(row_copies(stage + 1, (0, 3)))
        if which == 0 and stage < STAGES - 2:
            k = stage // 2
            partial[k : k + 1, :] = partial_sum + squares(own_edge - edge)
        if stage < STAGES - 2 and heard < levels:
            hear(heard)
            heard += 1
            tell(heard)

    store = pltpu.make_async_copy(result, out_ref, local.at[4])
    store.start()
    for stage in range(STAGES):
        depart(side_copies(stage))
        depart(row_copies(stage, (0, 1, 2, 3)))
    wait_all(gather_rows, rows - 1, norm_send.at[0])
    wait_all(gather_cols, cols - 1, norm_recv.at[1])
    total = gather_cols[0]
    for c in range(1, cols):
        total = total + gather_cols[c]
    sums = jnp.sum(total, axis=1, keepdims=True)
    place = lax.broadcasted_iota(jnp.int32, (1, 2), 1)
    norms_ref[...] = jnp.where(place == 0, sums[0:1], sums[1:2])
    wait_all(gather_cols, cols - 1, norm_send.at[1])
    store.wait()


def finish(estimate, norms, out, out_norms, block, small, loaded, stored):
    loads, stores = [], []
    height = 128 // 4
    for k in range(4):
        rows = pl.ds(height * k, height)
        loads.append(pltpu.make_async_copy(estimate.at[rows], block.at[rows], loaded.at[k]))
        stores.append(pltpu.make_async_copy(block.at[rows], out.at[rows], stored.at[k]))
    loads.append(pltpu.make_async_copy(norms, small, loaded.at[4]))
    stores.append(pltpu.make_async_copy(small, out_norms, stored.at[4]))
    for load in loads:
        load.start()
    for load, store in zip(loads, stores):
        load.wait()
        store.start()
    for store in stores:
        store.wait()


def body(rows, cols, observed, start, psf_rows, psf_cols):
    f32, bf16 = jnp.float32, jnp.bfloat16
    estimate, norms = pl.pallas_call(
        functools.partial(kernel, rows, cols),
        out_shape=(
            jax.ShapeDtypeStruct((128, 512), f32),
            jax.ShapeDtypeStruct((1, 2), f32),
        ),
        in_specs=[
            pl.BlockSpec(memory_space=pltpu.HBM),
            pl.BlockSpec(memory_space=pltpu.HBM),
            pl.BlockSpec(memory_space=pltpu.HBM),
            pl.BlockSpec(memory_space=pltpu.HBM),
        ],
        out_specs=(
            pl.BlockSpec(memory_space=pl.ANY),
            pl.BlockSpec(memory_space=pltpu.VMEM),
        ),
        scratch_shapes=[
            pltpu.VMEM((STAGES, 256, 512), f32),
            pltpu.VMEM((STAGES, 128, 128), f32),
            pltpu.VMEM((STAGES, 128, 128), f32),
            pltpu.VMEM((STAGES, 64, 128), f32),
            pltpu.VMEM((STAGES, 64, 128), f32),
            pltpu.VMEM((128, 512), f32),
            pltpu.VMEM((128, 512), f32),
            pltpu.VMEM((1, 127), f32),
            pltpu.VMEM((1, 127), f32),
            pltpu.VMEM((8, 256), f32),
            pltpu.VMEM((2, 256, 256), bf16),
            pltpu.VMEM((2, 256, 256), bf16),
            pltpu.VMEM((2, 128), f32),
            pltpu.VMEM((rows, 2, 128), f32),
            pltpu.VMEM((2, 128), f32),
            pltpu.VMEM((cols, 2, 128), f32),
            pltpu.SemaphoreType.DMA((STAGES, 6)),
            pltpu.SemaphoreType.DMA((STAGES, 6)),
            pltpu.SemaphoreType.DMA((STAGES, 2, 4)),
            pltpu.SemaphoreType.DMA((STAGES, 2, 4)),
            pltpu.SemaphoreType.DMA((5,)),
            pltpu.SemaphoreType.DMA((2,)),
            pltpu.SemaphoreType.DMA((2,)),
            pltpu.SemaphoreType.REGULAR((max(doublings(rows), doublings(cols)), 2)),
        ],
        compiler_params=pltpu.CompilerParams(
            collective_id=0, has_side_effects=True, vmem_limit_bytes=60 * 1024 * 1024
        ),
        name="deconvolve",
    )(observed[0], start[0], psf_rows.reshape(1, 127), psf_cols.reshape(1, 127))
    estimate, norms = pl.pallas_call(
        finish,
        out_shape=(jax.ShapeDtypeStruct((128, 512), f32), jax.ShapeDtypeStruct((1, 2), f32)),
        in_specs=[pl.BlockSpec(memory_space=pl.ANY)] * 2,
        out_specs=[pl.BlockSpec(memory_space=pl.ANY)] * 2,
        scratch_shapes=[
            pltpu.VMEM((128, 512), f32),
            pltpu.VMEM((1, 2), f32),
            pltpu.SemaphoreType.DMA((4 + 1,)),
            pltpu.SemaphoreType.DMA((4 + 1,)),
        ],
        compiler_params=pltpu.CompilerParams(vmem_limit_bytes=60 * 1024 * 1024),
        name="finish",
    )(estimate, norms)
    return estimate[None], norms.reshape(2)


def solution(mesh):
    in_specs = (P(None, "row", "col"), P(None, "row", "col"), P(), P())
    out_specs = (P(None, "row", "col"), P())
    step = functools.partial(body, mesh.shape["row"], mesh.shape["col"])
    return jax.shard_map(step, mesh=mesh, in_specs=in_specs, out_specs=out_specs, check_vma=False)
```

time: 48.9 us -> 46.2 us (0.945)
  local copies, waits for them, and re-layouts: 3.77 us -> 0 us
  Pallas kernels: 43.8 us -> 45.4 us
    unnamed x10 -> x0, local copies, waits for them, and re-layouts: 3.77 us -> none
    pallas_call x0 -> x1, Pallas kernels: none -> 1.65 us  [body(): pl.pallas_call(finish, out_shape=(jax.ShapeDtypeStruct((128, 512), f32),...]
where the time goes in v2:
time: 46.2 us; the launch traced here: 46 us
  Pallas kernels  45.4 us (98%)
  between operations  0.64 us (1%)
    pallas_call x1, Pallas kernels, body(): pl.pallas_call(functools.partial(kernel, rows, cols), out_shape=(jax.Shap...  43.7 us
    pallas_call x1, Pallas kernels, body(): pl.pallas_call(finish, out_shape=(jax.ShapeDtypeStruct((128, 512), f32),...  1.65 us

profile of v2, /device:TPU:1, one launch (start us, length us, event | category | flops | bytes accessed | tf_op | source)
XLA Modules:
  0.0 46.0 jit_solution(11718728462535505081)
XLA Ops:
  0.6 43.7 %deconvolve.1 = (f32[128,512]{1,0:T(8,128)}, f32[1,2]{1,0:T(1,128)}) custom-call(f32[128,512]{1,0:T(8,128)} %bitcast.6, f32[128,512]{1,0:T(8,128)} %bitcast.7, f32[1,127]{1,0:T(1,128)} %bitcast.8, f32[1,127]{1,0:T(1,128)} %bitcast.9), custom_call_target="tpu_custom_call" | custom-call | tf_op jit(solution)/shard_map/deconvolve/pallas_call | solution.py:392
  44.4 1.7 %finish.1 = (f32[128,512]{1,0:T(8,128)}, f32[1,2]{1,0:T(1,128)}) custom-call(f32[128,512]{1,0:T(8,128)} %get-tuple-element.6.estimate, f32[1,2]{1,0:T(1,128)} %get-tuple-element.7.norms), custom_call_target="tpu_custom_call" | custom-call | tf_op jit(solution)/shard_map/finish/pallas_call | solution.py:439

commit v3 on v2

--- a/solution.py
+++ b/solution.py
@@ -7,8 +7,6 @@
 from jax.experimental.pallas import tpu as pltpu
 from jax.sharding import PartitionSpec as P
 
-ITERS = 2
-STAGES = 2 * ITERS
 MESH = pl.DeviceIdType.MESH
 SIDES = ((-1, -1), (-1, 1), (1, -1), (1, 1), (0, -1), (0, 1))
 ENDS = ((-1, 0), (1, 0))
@@ -35,7 +33,8 @@
 
 def kernel(
     rows, cols, obs_hbm, start_hbm, rows_hbm, cols_hbm, out_ref, norms_ref,
-    field, left, right, pack_left, pack_right, seen, result, taps_rows, taps_cols, taps,
+    field, left, right, pack_left, pack_right, beside, ratio, deep_left, deep_right,
+    seen, result, taps_rows, taps_cols, taps,
     row_mats, col_mats, partial, gather_rows, middle, gather_cols,
     send_sides, recv_sides, send_rows, recv_rows, local, norm_send, norm_recv, known,
 ):
@@ -69,6 +68,7 @@
 
     lane = lax.broadcasted_iota(jnp.int32, (32, 128), 1) < 64
     lane_tall = lax.broadcasted_iota(jnp.int32, (128, 128), 1) < 64
+    lane_deep = lax.broadcasted_iota(jnp.int32, (256, 128), 1) < 64
 
     def remote(step, source, target, sent, received):
         inside, device = near(step)
@@ -82,21 +82,21 @@
         )
         return step, inside, copy
 
-    def side_copies(stage):
+    def side_copies(turn):
         ends = {
-            (0, -1): (pack_left.at[stage], right.at[stage, pl.ds(32, 64)]),
-            (0, 1): (pack_right.at[stage], left.at[stage, pl.ds(32, 64)]),
-            (-1, -1): (pack_left.at[stage, pl.ds(0, 32)], right.at[stage, pl.ds(96, 32)]),
-            (-1, 1): (pack_right.at[stage, pl.ds(0, 32)], left.at[stage, pl.ds(96, 32)]),
-            (1, -1): (pack_left.at[stage, pl.ds(32, 32)], right.at[stage, pl.ds(0, 32)]),
-            (1, 1): (pack_right.at[stage, pl.ds(32, 32)], left.at[stage, pl.ds(0, 32)]),
+            (0, -1): (pack_left.at[turn], right.at[turn, pl.ds(32, 64)]),
+            (0, 1): (pack_right.at[turn], left.at[turn, pl.ds(32, 64)]),
+            (-1, -1): (pack_left.at[turn, pl.ds(0, 32)], right.at[turn, pl.ds(96, 32)]),
+            (-1, 1): (pack_right.at[turn, pl.ds(0, 32)], left.at[turn, pl.ds(96, 32)]),
+            (1, -1): (pack_left.at[turn, pl.ds(32, 32)], right.at[turn, pl.ds(0, 32)]),
+            (1, 1): (pack_right.at[turn, pl.ds(32, 32)], left.at[turn, pl.ds(0, 32)]),
         }
         return [
-            remote(step, *ends[step], send_sides.at[stage, k], recv_sides.at[stage, k])
+            remote(step, *ends[step], send_sides.at[turn, k], recv_sides.at[turn, k])
             for k, step in enumerate(SIDES)
         ]
 
-    def row_copies(stage, blocks):
+    def row_copies(turn, blocks):
         made = []
         for k, step in enumerate(ENDS):
             source, target = ((64, 192), (128, 0))[k]
@@ -105,14 +105,45 @@
                 made.append(
                     remote(
                         step,
-                        field.at[stage, pl.ds(source, 64), lanes],
-                        field.at[stage, pl.ds(target, 64), lanes],
-                        send_rows.at[stage, k, b],
-                        recv_rows.at[stage, k, b],
+                        field.at[2 * turn, pl.ds(source, 64), lanes],
+                        field.at[2 * turn, pl.ds(target, 64), lanes],
+                        send_rows.at[turn, k, b],
+                        recv_rows.at[turn, k, b],
                     )
                 )
         return made
 
+    def deep_side_copies():
+        made = []
+        for k, (down, across) in enumerate(SIDES):
+            block, target = (0, deep_right) if across < 0 else (3, deep_left)
+            made.append(
+                remote(
+                    (down, across),
+                    ratio.at[pl.ds(128, 128), pl.ds(128 * block, 128)],
+                    target.at[pl.ds(128 - 128 * down, 128)],
+                    send_sides.at[2, k],
+                    recv_sides.at[2, k],
+                )
+            )
+        return made
+
+    def deep_row_copies(blocks):
+        made = []
+        for k, step in enumerate(ENDS):
+            for b in blocks:
+                lanes = pl.ds(128 * b, 128)
+                made.append(
+                    remote(
+                        step,
+                        ratio.at[pl.ds(128, 128), lanes],
+                        ratio.at[pl.ds(128 - 128 * step[0], 128), lanes],
+                        send_rows.at[2, k, b],
+                        recv_rows.at[2, k, b],
+                    )
+                )
+        return made
+
     def start(copies):
         for _, inside, copy in copies:
 
@@ -135,13 +166,13 @@
             def _():
                 copy.wait_send()
 
-    def pack(stage, edge):
+    def pack(turn, edge):
         for half in range(2):
             first = edge[64 * half : 64 * half + 32]
             second = pltpu.roll(edge[64 * half + 32 : 64 * half + 64], 64, 1)
             rows_here = slice(32 * half, 32 * half + 32)
-            pack_left[stage, rows_here, :] = jnp.where(lane, first, second)
-            pack_right[stage, rows_here, :] = jnp.where(lane, second, first)
+            pack_left[turn, rows_here, :] = jnp.where(lane, first, second)
+            pack_right[turn, rows_here, :] = jnp.where(lane, second, first)
 
     def along_rows(which, value):
         high, low = split(value)
@@ -149,26 +180,33 @@
         return both[0:128] + both[128:256] + dot(row_mats[which, 0:128, :], low)
 
     def along_cols(which, blocks, first, second):
-        nothing = jnp.zeros((128, 128), jnp.float32)
+        height = blocks[first].shape[0]
+        low_lanes = lane_tall if height == 128 else lane_deep
+        nothing = jnp.zeros((height, 128), jnp.float32)
         pairs = []
         for b in (first, second):
-            mixed = jnp.where(lane_tall, blocks.get(b + 1, nothing), blocks.get(b - 1, nothing))
+            mixed = jnp.where(low_lanes, blocks.get(b + 1, nothing), blocks.get(b - 1, nothing))
             pairs.append(jnp.concatenate([blocks[b], mixed], axis=1))
         high, low = split(jnp.concatenate(pairs, axis=0))
         both = dot(high, col_mats[which])
         flat = both[:, 0:128] + both[:, 128:256] + dot(low, col_mats[which, :, 0:128])
-        return flat[0:128], flat[128:256]
+        return flat[0:height], flat[height : 2 * height]
 
     def along_cols_edge(which, halo):
         high, low = split(halo)
         both = dot(high, col_mats[which, 128:256, :])
         return both[:, 0:128] + both[:, 128:256] + dot(low, col_mats[which, 128:256, 0:128])
 
-    def sides(stage):
+    def along_rows_deep(which, value):
+        return jnp.concatenate(
+            [along_rows(which, value[0:256]), along_rows(which, value[128:384])], axis=0
+        )
+
+    def sides(turn):
         parts = []
         for group in range(4):
-            from_left = left[stage, 32 * group : 32 * group + 32, :]
-            from_right = right[stage, 32 * group : 32 * group + 32, :]
+            from_left = left[turn, 32 * group : 32 * group + 32, :]
+            from_right = right[turn, 32 * group : 32 * group + 32, :]
             parts.append(jnp.where(lane, from_right, from_left))
             parts.append(pltpu.roll(jnp.where(lane, from_left, from_right), 64, 1))
         return jnp.concatenate(parts, axis=0)
@@ -238,23 +276,33 @@
 
     @pl.when(row == 0)
     def _():
-        field[:, 0:64, :] = jnp.zeros((STAGES, 64, 512), jnp.float32)
-        left[:, 0:32, :] = jnp.zeros((STAGES, 32, 128), jnp.float32)
-        right[:, 0:32, :] = jnp.zeros((STAGES, 32, 128), jnp.float32)
+        for k in (0, 2):
+            field[k, 0:64, :] = jnp.zeros((64, 512), jnp.float32)
+        ratio[0:128, :] = jnp.zeros((128, 512), jnp.float32)
+        for buffer in (left, right):
+            buffer[:, 0:32, :] = jnp.zeros((2, 32, 128), jnp.float32)
+        for buffer in (deep_left, deep_right):
+            buffer[0:128, :] = jnp.zeros((128, 128), jnp.float32)
 
     @pl.when(row == rows - 1)
     def _():
-        field[:, 192:256, :] = jnp.zeros((STAGES, 64, 512), jnp.float32)
-        left[:, 96:128, :] = jnp.zeros((STAGES, 32, 128), jnp.float32)
-        right[:, 96:128, :] = jnp.zeros((STAGES, 32, 128), jnp.float32)
+        for k in (0, 2):
+            field[k, 192:256, :] = jnp.zeros((64, 512), jnp.float32)
+        ratio[256:384, :] = jnp.zeros((128, 512), jnp.float32)
+        for buffer in (left, right):
+            buffer[:, 96:128, :] = jnp.zeros((2, 32, 128), jnp.float32)
+        for buffer in (deep_left, deep_right):
+            buffer[256:384, :] = jnp.zeros((128, 128), jnp.float32)
 
     @pl.when(col == 0)
     def _():
-        left[...] = jnp.zeros((STAGES, 128, 128), jnp.float32)
+        left[...] = jnp.zeros((2, 128, 128), jnp.float32)
+        deep_left[...] = jnp.zeros((384, 128), jnp.float32)
 
     @pl.when(col == cols - 1)
     def _():
-        right[...] = jnp.zeros((STAGES, 128, 128), jnp.float32)
+        right[...] = jnp.zeros((2, 128, 128), jnp.float32)
+        deep_right[...] = jnp.zeros((384, 128), jnp.float32)
 
     load_rows.wait()
     load_cols.wait()
@@ -274,89 +322,119 @@
         col_mats[which, :, 128:256] = low
     load_seen.wait()
 
-    def updated(stage, own, blurred):
-        return own / blurred if stage % 2 == 0 else own * blurred
-
-    levels = max(doublings(rows), doublings(cols))
-    hear(0)
-    tell(1)
-    heard = 1
-    for stage in range(STAGES):
-        which, last = stage % 2, stage + 1 == STAGES
-        if last:
-            wait_all(gather_rows, rows - 1, norm_recv.at[0])
-            total = gather_rows[0]
-            for r in range(1, rows):
-                total = total + gather_rows[r]
-            middle[...] = total
-            gather_cols[col] = total
-            lax.fori_loop(1, cols, start_norm_col, 0)
-
-        def own(b):
-            lanes = slice(128 * b, 128 * b + 128)
-            return seen[:, lanes] if which == 0 else field[stage - 1, 64:192, lanes]
-
-        def put(b, value):
-            lanes = slice(128 * b, 128 * b + 128)
-            if last:
-                result[:, lanes] = value
-            else:
-                field[stage + 1, 64:192, lanes] = value
-
-        blocks, outs = {}, {}
-        arrive(row_copies(stage, (1, 2)))
-        both = along_rows(which, field[stage, :, 128:384])
-        blocks[1], blocks[2] = both[:, 0:128], both[:, 128:256]
-        arrive(row_copies(stage, (0, 3)))
-        both = along_rows(
-            which, jnp.concatenate([field[stage, :, 0:128], field[stage, :, 384:512]], axis=1)
-        )
-        blocks[0], blocks[3] = both[:, 0:128], both[:, 128:256]
-        outs[1], outs[2] = along_cols(which, blocks, 1, 2)
-        for b in (1, 2):
-            put(b, updated(stage, own(b), outs[b]))
-        if not last:
-            start(row_copies(stage + 1, (1, 2)))
-        outs[0], outs[3] = along_cols(which, blocks, 0, 3)
-        inner = {b: updated(stage, own(b), outs[b]) for b in (0, 3)}
-        if which == 0:
-            partial_sum = squares(own(1) - outs[1]) + squares(own(2) - outs[2])
-            partial_sum = partial_sum + squares(
-                jnp.where(lane_tall, own(3) - outs[3], own(0) - outs[0])
-            )
-        own_edge = jnp.where(lane_tall, own(0), own(3))
-        edge = jnp.where(lane_tall, outs[0], outs[3])
-        if stage > 0 and heard < levels:
-            hear(heard)
-            heard += 1
-            tell(heard)
-        arrive(side_copies(stage))
-        edge = edge + along_cols_edge(which, along_rows(which, sides(stage)))
-        if stage == STAGES - 2:
-            partial[ITERS - 1 : ITERS, :] = partial_sum + squares(own_edge - edge)
-            gather_rows[row] = partial[...]
-            lax.fori_loop(1, rows, start_norm_row, 0)
-        outer = updated(stage, own_edge, edge)
-        if not last:
-            pack(stage + 1, outer)
-            start(side_copies(stage + 1))
-        put(0, jnp.where(lane_tall, outer, inner[0]))
-        put(3, jnp.where(lane_tall, inner[3], outer))
-        if not last:
-            start(row_copies(stage + 1, (0, 3)))
-        if which == 0 and stage < STAGES - 2:
-            k = stage // 2
-            partial[k : k + 1, :] = partial_sum + squares(own_edge - edge)
-        if stage < STAGES - 2 and heard < levels:
-            hear(heard)
-            heard += 1
-            tell(heard)
+    def at(b):
+        return slice(128 * b, 128 * b + 128)
+
+    def pair(value):
+        return value[:, 0:128], value[:, 128:256]
+
+    def outer_blocks(value):
+        return jnp.concatenate([value[:, 0:128], value[:, 384:512]], axis=1)
+
+    rounds = max(doublings(rows), doublings(cols))
+
+    def spread(level):
+        if level < rounds:
+            hear(level)
+            tell(level + 1)
+
+    spread(0)
+
+    blocks, outs = {}, {}
+    arrive(row_copies(0, (1, 2)))
+    blocks[1], blocks[2] = pair(along_rows(0, field[0, :, 128:384]))
+    arrive(row_copies(0, (0, 3)))
+    blocks[0], blocks[3] = pair(along_rows(0, outer_blocks(field[0])))
+    outs[1], outs[2] = along_cols(0, blocks, 1, 2)
+    for b in (1, 2):
+        ratio[128:256, at(b)] = seen[:, at(b)] / outs[b]
+    start(deep_row_copies((1, 2)))
+    outs[0], outs[3] = along_cols(0, blocks, 0, 3)
+    seen_edge = jnp.where(lane_tall, seen[:, at(0)], seen[:, at(3)])
+    edge = jnp.where(lane_tall, outs[0], outs[3])
+    for b in (0, 3):
+        ratio[128:256, at(b)] = seen[:, at(b)] / outs[b]
+    inner_sum = squares(seen[:, at(1)] - outs[1]) + squares(seen[:, at(2)] - outs[2])
+    inner_sum = inner_sum + squares(
+        jnp.where(lane_tall, seen[:, at(3)] - outs[3], seen[:, at(0)] - outs[0])
+    )
+    spread(1)
+    arrive(side_copies(0))
+    halo = sides(0)
+    beside[...] = halo
+    edge = edge + along_cols_edge(0, along_rows(0, halo))
+    outer = seen_edge / edge
+    ratio[128:256, at(0)] = jnp.where(lane_tall, outer, ratio[128:256, at(0)])
+    ratio[128:256, at(3)] = jnp.where(lane_tall, ratio[128:256, at(3)], outer)
+    start(deep_side_copies())
+    start(deep_row_copies((0, 3)))
+    partial[0:1, :] = inner_sum + squares(seen_edge - edge)
+    spread(2)
+    spread(3)
+
+    blocks, outs = {}, {}
+    arrive(deep_row_copies((1, 2)))
+    blocks[1], blocks[2] = pair(along_rows_deep(1, ratio[:, 128:384]))
+    arrive(deep_row_copies((0, 3)))
+    blocks[0], blocks[3] = pair(along_rows_deep(1, outer_blocks(ratio)))
+    outs[1], outs[2] = along_cols(1, blocks, 1, 2)
+    for b in (1, 2):
+        field[1, :, at(b)] = field[0, :, at(b)] * outs[b]
+    outs[0], outs[3] = along_cols(1, blocks, 0, 3)
+    again = {}
+    again[1], again[2] = pair(along_rows(0, field[1, :, 128:384]))
+    for level in range(4, rounds):
+        spread(level)
+    arrive(deep_side_copies())
+    blocks[-1], blocks[4] = pair(
+        along_rows_deep(1, jnp.concatenate([deep_left[...], deep_right[...]], axis=1))
+    )
+    edge = along_cols_edge(1, jnp.where(lane_deep, blocks[4], blocks[-1]))
+    outs[-1], outs[4] = along_cols(1, blocks, -1, 4)
+    field[1, :, at(0)] = field[0, :, at(0)] * jnp.where(lane_deep, outs[0] + edge, outs[0])
+    field[1, :, at(3)] = field[0, :, at(3)] * jnp.where(lane_deep, outs[3], outs[3] + edge)
+    halo = beside[...] * jnp.where(lane_deep, outs[4], outs[-1])
+
+    again[0], again[3] = pair(along_rows(0, outer_blocks(field[1])))
+    again[-1] = again[4] = along_rows(0, halo)
+    outs = {}
+    outs[0], outs[3] = along_cols(0, again, 0, 3)
+    outs[1], outs[2] = along_cols(0, again, 1, 2)
+    partial[1:2, :] = sum(squares(seen[:, at(b)] - outs[b]) for b in range(4))
+    gather_rows[row] = partial[...]
+    lax.fori_loop(1, rows, start_norm_row, 0)
+    for b in range(4):
+        field[2, 64:192, at(b)] = seen[:, at(b)] / outs[b]
+    pack(1, jnp.where(lane_tall, field[2, 64:192, at(0)], field[2, 64:192, at(3)]))
+    start(side_copies(1))
+    start(row_copies(1, (0, 1, 2, 3)))
+
+    wait_all(gather_rows, rows - 1, norm_recv.at[0])
+    total = gather_rows[0]
+    for r in range(1, rows):
+        total = total + gather_rows[r]
+    middle[...] = total
+    gather_cols[col] = total
+    lax.fori_loop(1, cols, start_norm_col, 0)
+
+    blocks, outs = {}, {}
+    arrive(row_copies(1, (0, 1, 2, 3)))
+    blocks[1], blocks[2] = pair(along_rows(1, field[2, :, 128:384]))
+    blocks[0], blocks[3] = pair(along_rows(1, outer_blocks(field[2])))
+    outs[1], outs[2] = along_cols(1, blocks, 1, 2)
+    arrive(side_copies(1))
+    blocks[-1] = blocks[4] = along_rows(1, sides(1))
+    outs[0], outs[3] = along_cols(1, blocks, 0, 3)
+    for b in range(4):
+        result[:, at(b)] = field[1, 64:192, at(b)] * outs[b]
 
     store = pltpu.make_async_copy(result, out_ref, local.at[4])
     store.start()
-    for stage in range(STAGES):
-        depart(side_copies(stage))
-        depart(row_copies(stage, (0, 1, 2, 3)))
+    for turn in range(2):
+        depart(side_copies(turn))
+        depart(row_copies(turn, (0, 1, 2, 3)))
+    depart(deep_side_copies())
+    depart(deep_row_copies((0, 1, 2, 3)))
     wait_all(gather_rows, rows - 1, norm_send.at[0])
     wait_all(gather_cols, cols - 1, norm_recv.at[1])
     total = gather_cols[0]
@@ -406,11 +484,15 @@
             pl.BlockSpec(memory_space=pltpu.VMEM),
         ),
         scratch_shapes=[
-            pltpu.VMEM((STAGES, 256, 512), f32),
-            pltpu.VMEM((STAGES, 128, 128), f32),
-            pltpu.VMEM((STAGES, 128, 128), f32),
-            pltpu.VMEM((STAGES, 64, 128), f32),
-            pltpu.VMEM((STAGES, 64, 128), f32),
+            pltpu.VMEM((3, 256, 512), f32),
+            pltpu.VMEM((2, 128, 128), f32),
+            pltpu.VMEM((2, 128, 128), f32),
+            pltpu.VMEM((2, 64, 128), f32),
+            pltpu.VMEM((2, 64, 128), f32),
+            pltpu.VMEM((256, 128), f32),
+            pltpu.VMEM((384, 512), f32),
+            pltpu.VMEM((384, 128), f32),
+            pltpu.VMEM((384, 128), f32),
             pltpu.VMEM((128, 512), f32),
             pltpu.VMEM((128, 512), f32),
             pltpu.VMEM((1, 127), f32),
@@ -422,10 +504,10 @@
             pltpu.VMEM((rows, 2, 128), f32),
             pltpu.VMEM((2, 128), f32),
             pltpu.VMEM((cols, 2, 128), f32),
-            pltpu.SemaphoreType.DMA((STAGES, 6)),
-            pltpu.SemaphoreType.DMA((STAGES, 6)),
-            pltpu.SemaphoreType.DMA((STAGES, 2, 4)),
-            pltpu.SemaphoreType.DMA((STAGES, 2, 4)),
+            pltpu.SemaphoreType.DMA((3, 6)),
+            pltpu.SemaphoreType.DMA((3, 6)),
+            pltpu.SemaphoreType.DMA((3, 2, 4)),
+            pltpu.SemaphoreType.DMA((3, 2, 4)),
             pltpu.SemaphoreType.DMA((5,)),
             pltpu.SemaphoreType.DMA((2,)),
             pltpu.SemaphoreType.DMA((2,)),

time: 46.2 us -> 44.4 us (0.961)
  Pallas kernels: 45.4 us -> 43.6 us
    pallas_call x1, Pallas kernels: 43.7 us -> 41.9 us  [body(): pl.pallas_call(functools.partial(kernel, rows, cols), out_shape=(jax.Shap...]
where the time goes in v3:
time: 44.4 us; the launch traced here: 44.2 us
  Pallas kernels  43.6 us (98%)
  between operations  0.64 us (1%)
    pallas_call x1, Pallas kernels, body(): pl.pallas_call(functools.partial(kernel, rows, cols), out_shape=(jax.Shap...  41.9 us
    pallas_call x1, Pallas kernels, body(): pl.pallas_call(finish, out_shape=(jax.ShapeDtypeStruct((128, 512), f32),...  1.65 us

profile of v3, /device:TPU:1, one launch (start us, length us, event | category | flops | bytes accessed | tf_op | source)
XLA Modules:
  0.0 44.2 jit_solution(12013977909001437656)
XLA Ops:
  0.6 41.9 %deconvolve.1 = (f32[128,512]{1,0:T(8,128)}, f32[1,2]{1,0:T(1,128)}) custom-call(f32[128,512]{1,0:T(8,128)} %bitcast.6, f32[128,512]{1,0:T(8,128)} %bitcast.7, f32[1,127]{1,0:T(1,128)} %bitcast.8, f32[1,127]{1,0:T(1,128)} %bitcast.9), custom_call_target="tpu_custom_call" | custom-call | tf_op jit(solution)/shard_map/deconvolve/pallas_call | solution.py:470
  42.5 1.7 %finish.1 = (f32[128,512]{1,0:T(8,128)}, f32[1,2]{1,0:T(1,128)}) custom-call(f32[128,512]{1,0:T(8,128)} %get-tuple-element.6.estimate, f32[1,2]{1,0:T(1,128)} %get-tuple-element.7.norms), custom_call_target="tpu_custom_call" | custom-call | tf_op jit(solution)/shard_map/finish/pallas_call | solution.py:521

commit v4 on v3

--- a/solution.py
+++ b/solution.py
@@ -8,6 +8,7 @@
 from jax.sharding import PartitionSpec as P
 
 MESH = pl.DeviceIdType.MESH
+EARLY = ((1, 0), (2, 0), (16, 0), (0, 1))
 SIDES = ((-1, -1), (-1, 1), (1, -1), (1, 1), (0, -1), (0, 1))
 ENDS = ((-1, 0), (1, 0))
 
@@ -35,7 +36,7 @@
     rows, cols, obs_hbm, start_hbm, rows_hbm, cols_hbm, out_ref, norms_ref,
     field, left, right, pack_left, pack_right, beside, ratio, deep_left, deep_right,
     seen, result, taps_rows, taps_cols, taps,
-    row_mats, col_mats, partial, gather_rows, middle, gather_cols,
+    row_mats, col_mats, partial, gather_rows, middle, gather_cols, gather_all,
     send_sides, recv_sides, send_rows, recv_rows, local, norm_send, norm_recv, known,
 ):
     row, col = lax.axis_index("row"), lax.axis_index("col")
@@ -61,6 +62,26 @@
             pl.semaphore_signal(barrier, inc=1, device_id=device, device_id_type=MESH)
 
         expected = expected + inside.astype(jnp.int32)
+
+    early = [(r, c) for r, c in EARLY if r < rows and c < cols]
+    is_early = [(row == r) & (col == c) for r, c in early]
+    for here in is_early:
+        @pl.when(here)
+        def _():
+            def greet(k, carry):
+                r, c = lax.rem(k, rows), cols - 1 - lax.div(k, rows)
+
+                @pl.when((r != row) | (c != col))
+                def _():
+                    pl.semaphore_signal(
+                        barrier, inc=1, device_id=(r, c), device_id_type=MESH
+                    )
+
+                return carry
+
+            lax.fori_loop(0, rows * cols, greet, 0)
+
+        expected = expected + (1 - here.astype(jnp.int32))
 
     load_seen.start()
     load_rows.start()
@@ -242,9 +263,33 @@
         norm_row(d).start()
         return carry
 
+    def served(r, c):
+        out = jnp.bool_(False)
+        for e in early:
+            out = out | ((r == e[0]) & (c == e[1]))
+        return out
+
     def start_norm_col(d, carry):
-        norm_col(d).start()
+        @pl.when(jnp.logical_not(served(row, lax.rem(col + d, cols))))
+        def _():
+            norm_col(d).start()
+
         return carry
+
+    def direct(k):
+        return pltpu.make_async_remote_copy(
+            src_ref=partial,
+            dst_ref=gather_all.at[row * cols + col],
+            send_sem=norm_send.at[2 + k],
+            recv_sem=norm_recv.at[2],
+            device_id=early[k],
+            device_id_type=MESH,
+        )
+
+    am_early = served(row, col)
+    one_less = jnp.bool_(False)
+    for e in early:
+        one_less = one_less | ((row == e[0]) & (col != e[1]))
 
     def tell(level):
         for k, steps in enumerate(((1, 0), (0, 1))):
@@ -368,7 +413,8 @@
     ratio[128:256, at(3)] = jnp.where(lane_tall, ratio[128:256, at(3)], outer)
     start(deep_side_copies())
     start(deep_row_copies((0, 3)))
-    partial[0:1, :] = inner_sum + squares(seen_edge - edge)
+    first_norm = inner_sum + squares(seen_edge - edge)
+    first_norm = first_norm + pltpu.roll(first_norm, 64, 1)
     spread(2)
     spread(3)
 
@@ -400,8 +446,20 @@
     outs = {}
     outs[0], outs[3] = along_cols(0, again, 0, 3)
     outs[1], outs[2] = along_cols(0, again, 1, 2)
-    partial[1:2, :] = sum(squares(seen[:, at(b)] - outs[b]) for b in range(4))
+    last_norm = sum(squares(seen[:, at(b)] - outs[b]) for b in range(4))
+    last_norm = last_norm + pltpu.roll(last_norm, 64, 1)
+    partial[...] = jnp.where(lane[0:1], first_norm, last_norm)
     gather_rows[row] = partial[...]
+    for k, here in enumerate(is_early):
+
+        @pl.when(here)
+        def _():
+            gather_all[row * cols + col] = partial[...]
+
+        @pl.when(jnp.logical_not(here))
+        def _():
+            direct(k).start()
+
     lax.fori_loop(1, rows, start_norm_row, 0)
     for b in range(4):
         field[2, 64:192, at(b)] = seen[:, at(b)] / outs[b]
@@ -436,14 +494,46 @@
     depart(deep_side_copies())
     depart(deep_row_copies((0, 1, 2, 3)))
     wait_all(gather_rows, rows - 1, norm_send.at[0])
-    wait_all(gather_cols, cols - 1, norm_recv.at[1])
-    total = gather_cols[0]
-    for c in range(1, cols):
-        total = total + gather_cols[c]
-    sums = jnp.sum(total, axis=1, keepdims=True)
     place = lax.broadcasted_iota(jnp.int32, (1, 2), 1)
-    norms_ref[...] = jnp.where(place == 0, sums[0:1], sums[1:2])
-    wait_all(gather_cols, cols - 1, norm_send.at[1])
+
+    def put_norms(total):
+        first = jnp.sum(jnp.where(lane[0:1], total, 0.0), axis=1, keepdims=True)
+        last = jnp.sum(jnp.where(lane[0:1], 0.0, total), axis=1, keepdims=True)
+        norms_ref[...] = jnp.where(place == 0, first, last)
+
+    @pl.when(am_early)
+    def _():
+        wait_all(gather_all, rows * cols - 1, norm_recv.at[2])
+        total = None
+        for c in range(cols):
+            part = gather_all[c]
+            for r in range(1, rows):
+                part = part + gather_all[r * cols + c]
+            total = part if total is None else total + part
+        put_norms(total)
+
+    @pl.when(jnp.logical_not(am_early))
+    def _():
+        wait_all(gather_cols, cols - 1, norm_recv.at[1])
+        total = gather_cols[0]
+        for c in range(1, cols):
+            total = total + gather_cols[c]
+        put_norms(total)
+
+    @pl.when(one_less)
+    def _():
+        wait_all(gather_cols, cols - 2, norm_send.at[1])
+
+    @pl.when(jnp.logical_not(one_less))
+    def _():
+        wait_all(gather_cols, cols - 1, norm_send.at[1])
+
+    for k, here in enumerate(is_early):
+
+        @pl.when(jnp.logical_not(here))
+        def _():
+            direct(k).wait_send()
+
     store.wait()
 
 
@@ -500,17 +590,18 @@
             pltpu.VMEM((8, 256), f32),
             pltpu.VMEM((2, 256, 256), bf16),
             pltpu.VMEM((2, 256, 256), bf16),
-            pltpu.VMEM((2, 128), f32),
-            pltpu.VMEM((rows, 2, 128), f32),
-            pltpu.VMEM((2, 128), f32),
-            pltpu.VMEM((cols, 2, 128), f32),
+            pltpu.VMEM((1, 128), f32),
+            pltpu.VMEM((rows, 1, 128), f32),
+            pltpu.VMEM((1, 128), f32),
+            pltpu.VMEM((cols, 1, 128), f32),
+            pltpu.VMEM((rows * cols, 1, 128), f32),
             pltpu.SemaphoreType.DMA((3, 6)),
             pltpu.SemaphoreType.DMA((3, 6)),
             pltpu.SemaphoreType.DMA((3, 2, 4)),
             pltpu.SemaphoreType.DMA((3, 2, 4)),
             pltpu.SemaphoreType.DMA((5,)),
-            pltpu.SemaphoreType.DMA((2,)),
-            pltpu.SemaphoreType.DMA((2,)),
+            pltpu.SemaphoreType.DMA((2 + len(EARLY),)),
+            pltpu.SemaphoreType.DMA((3,)),
             pltpu.SemaphoreType.REGULAR((max(doublings(rows), doublings(cols)), 2)),
         ],
         compiler_params=pltpu.CompilerParams(

time: 44.4 us -> 42.4 us (0.955)
  Pallas kernels: 43.6 us -> 41.4 us
    pallas_call x1, Pallas kernels: 41.9 us -> 39.7 us  [body(): pl.pallas_call(functools.partial(kernel, rows, cols), out_shape=(jax.Shap...]
where the time goes in v4:
time: 42.4 us; the launch traced here: 42 us
  Pallas kernels  41.4 us (98%)
  between operations  0.64 us (2%)
    pallas_call x1, Pallas kernels, body(): pl.pallas_call(functools.partial(kernel, rows, cols), out_shape=(jax.Shap...  39.7 us
    pallas_call x1, Pallas kernels, body(): pl.pallas_call(finish, out_shape=(jax.ShapeDtypeStruct((128, 512), f32),...  1.65 us

profile of v4, /device:TPU:1, one launch (start us, length us, event | category | flops | bytes accessed | tf_op | source)
XLA Modules:
  0.0 42.0 jit_solution(12523248016552204594)
XLA Ops:
  0.6 39.7 %deconvolve.1 = (f32[128,512]{1,0:T(8,128)}, f32[1,2]{1,0:T(1,128)}) custom-call(f32[128,512]{1,0:T(8,128)} %bitcast.6, f32[128,512]{1,0:T(8,128)} %bitcast.7, f32[1,127]{1,0:T(1,128)} %bitcast.8, f32[1,127]{1,0:T(1,128)} %bitcast.9), custom_call_target="tpu_custom_call" | custom-call | tf_op jit(solution)/shard_map/deconvolve/pallas_call | solution.py:560
  40.3 1.7 %finish.1 = (f32[128,512]{1,0:T(8,128)}, f32[1,2]{1,0:T(1,128)}) custom-call(f32[128,512]{1,0:T(8,128)} %get-tuple-element.6.estimate, f32[1,2]{1,0:T(1,128)} %get-tuple-element.7.norms), custom_call_target="tpu_custom_call" | custom-call | tf_op jit(solution)/shard_map/finish/pallas_call | solution.py:612

commit v5 on v4

--- a/solution.py
+++ b/solution.py
@@ -537,22 +537,15 @@
     store.wait()
 
 
-def finish(estimate, norms, out, out_norms, block, small, loaded, stored):
-    loads, stores = [], []
-    height = 128 // 4
-    for k in range(4):
-        rows = pl.ds(height * k, height)
-        loads.append(pltpu.make_async_copy(estimate.at[rows], block.at[rows], loaded.at[k]))
-        stores.append(pltpu.make_async_copy(block.at[rows], out.at[rows], stored.at[k]))
-    loads.append(pltpu.make_async_copy(norms, small, loaded.at[4]))
-    stores.append(pltpu.make_async_copy(small, out_norms, stored.at[4]))
-    for load in loads:
-        load.start()
-    for load, store in zip(loads, stores):
-        load.wait()
-        store.start()
-    for store in stores:
-        store.wait()
+def finish(estimate, norms, out, out_norms, done):
+    copies = (
+        pltpu.make_async_copy(estimate, out, done.at[0]),
+        pltpu.make_async_copy(norms, out_norms, done.at[1]),
+    )
+    for copy in copies:
+        copy.start()
+    for copy in copies:
+        copy.wait()
 
 
 def body(rows, cols, observed, start, psf_rows, psf_cols):
@@ -605,7 +598,7 @@
             pltpu.SemaphoreType.REGULAR((max(doublings(rows), doublings(cols)), 2)),
         ],
         compiler_params=pltpu.CompilerParams(
-            collective_id=0, has_side_effects=True, vmem_limit_bytes=60 * 1024 * 1024
+            collective_id=0, has_side_effects=True, vmem_limit_bytes=54850 * 1024
         ),
         name="deconvolve",
     )(observed[0], start[0], psf_rows.reshape(1, 127), psf_cols.reshape(1, 127))
@@ -615,12 +608,9 @@
         in_specs=[pl.BlockSpec(memory_space=pl.ANY)] * 2,
         out_specs=[pl.BlockSpec(memory_space=pl.ANY)] * 2,
         scratch_shapes=[
-            pltpu.VMEM((128, 512), f32),
-            pltpu.VMEM((1, 2), f32),
-            pltpu.SemaphoreType.DMA((4 + 1,)),
-            pltpu.SemaphoreType.DMA((4 + 1,)),
+            pltpu.SemaphoreType.DMA((2,)),
         ],
-        compiler_params=pltpu.CompilerParams(vmem_limit_bytes=60 * 1024 * 1024),
+        compiler_params=pltpu.CompilerParams(vmem_limit_bytes=54850 * 1024),
         name="finish",
     )(estimate, norms)
     return estimate[None], norms.reshape(2)

time: 42.4 us -> 41.7 us (0.983)
  Pallas kernels: 41.4 us -> 39.9 us
  local copies, waits for them, and re-layouts: 0 us -> 0.66 us
    pallas_call x1, Pallas kernels: 1.65 us -> 0.72 us  [body(): pl.pallas_call(finish, out_shape=(jax.ShapeDtypeStruct((128, 512), f32),...]
    unnamed x0 -> x4, local copies, waits for them, and re-layouts: none -> 0.66 us
    pallas_call x1, Pallas kernels: 39.7 us -> 39.2 us  [body(): pl.pallas_call(functools.partial(kernel, rows, cols), out_shape=(jax.Shap...]
where the time goes in v5:
time: 41.7 us; the launch traced here: 41.3 us
  Pallas kernels  39.9 us (96%)
  local copies, waits for them, and re-layouts  0.66 us (2%)
  between operations  0.66 us (2%)
    pallas_call x1, Pallas kernels, body(): pl.pallas_call(functools.partial(kernel, rows, cols), out_shape=(jax.Shap...  39.2 us

profile of v5, /device:TPU:1, one launch (start us, length us, event | category | flops | bytes accessed | tf_op | source)
XLA Modules:
  0.0 41.3 jit_solution(2763429111447967401)
XLA Ops:
  0.6 0.0 copy-start
  0.6 0.0 copy-start.1
  0.7 0.6 %copy-done = f32[127]{0:T(128)S(1)} copy-done((f32[127]{0:T(128)S(1)}, f32[127]{0:T(128)}, u32[]{:S(2)}) %copy-start) | copy-done | bytes 532
  1.3 0.0 copy-done.1
  1.3 39.2 %deconvolve.1 = (f32[128,512]{1,0:T(8,128)S(1)}, f32[1,2]{1,0:T(1,128)S(1)}) custom-call(f32[128,512]{1,0:T(8,128)} %bitcast.8, f32[128,512]{1,0:T(8,128)} %bitcast.9, f32[1,127]{1,0:T(1,128)S(1)} %bitcast.6, f32[1,127]{1,0:T(1,128)S(1)} %bitcast.7), custom_call_target="tpu_custom_call" | custom-call | tf_op jit(solution)/shard_map/deconvolve/pallas_call | solution.py:553
  40.5 0.7 %finish.1 = (f32[128,512]{1,0:T(8,128)}, f32[1,2]{1,0:T(1,128)}) custom-call(f32[128,512]{1,0:T(8,128)S(1)} %get-tuple-element.6.estimate, f32[1,2]{1,0:T(1,128)S(1)} %get-tuple-element.7.norms), custom_call_target="tpu_custom_call" | custom-call | tf_op jit(solution)/shard_map/finish/pallas_call | solution.py:605
Async XLA Ops:
  0.6 0.7 %copy-start = (f32[127]{0:T(128)S(1)}, f32[127]{0:T(128)}, u32[]{:S(2)}) copy-start(f32[127]{0:T(128)} %param.6) | copy-start | bytes 1528
  0.6 0.7 %copy-start.1 = (f32[127]{0:T(128)S(1)}, f32[127]{0:T(128)}, u32[]{:S(2)}) copy-start(f32[127]{0:T(128)} %param.7) | copy-start | bytes 1528

commit v6 on v5

--- a/solution.py
+++ b/solution.py
@@ -117,22 +117,17 @@
             for k, step in enumerate(SIDES)
         ]
 
-    def row_copies(turn, blocks):
-        made = []
-        for k, step in enumerate(ENDS):
-            source, target = ((64, 192), (128, 0))[k]
-            for b in blocks:
-                lanes = pl.ds(128 * b, 128)
-                made.append(
-                    remote(
-                        step,
-                        field.at[2 * turn, pl.ds(source, 64), lanes],
-                        field.at[2 * turn, pl.ds(target, 64), lanes],
-                        send_rows.at[turn, k, b],
-                        recv_rows.at[turn, k, b],
-                    )
-                )
-        return made
+    def row_copies(turn):
+        return [
+            remote(
+                step,
+                field.at[2 * turn, pl.ds(source, 64)],
+                field.at[2 * turn, pl.ds(target, 64)],
+                send_rows.at[turn, k, 0],
+                recv_rows.at[turn, k, 0],
+            )
+            for k, (step, source, target) in enumerate(((ENDS[0], 64, 192), (ENDS[1], 128, 0)))
+        ]
 
     def deep_side_copies():
         made = []
@@ -165,27 +160,36 @@
                 )
         return made
 
+    def by_step(copies):
+        groups = {}
+        for step, inside, copy in copies:
+            groups.setdefault(step, (inside, []))[1].append(copy)
+        return groups.items()
+
     def start(copies):
-        for _, inside, copy in copies:
+        for _, (inside, group) in by_step(copies):
 
             @pl.when(inside)
             def _():
-                copy.start()
+                for copy in group:
+                    copy.start()
 
     def arrive(copies):
-        for step, _, copy in copies:
+        for step, (_, group) in by_step(copies):
             inside, _ = near((-step[0], -step[1]))
 
             @pl.when(inside)
             def _():
-                copy.wait_recv()
+                for copy in group:
+                    copy.wait_recv()
 
     def depart(copies):
-        for _, inside, copy in copies:
+        for _, (inside, group) in by_step(copies):
 
             @pl.when(inside)
             def _():
-                copy.wait_send()
+                for copy in group:
+                    copy.wait_send()
 
     def pack(turn, edge):
         for half in range(2):
@@ -200,18 +204,18 @@
         both = dot(row_mats[which], high)
         return both[0:128] + both[128:256] + dot(row_mats[which, 0:128, :], low)
 
-    def along_cols(which, blocks, first, second):
-        height = blocks[first].shape[0]
+    def along_cols(which, blocks, *wanted):
+        height = blocks[wanted[0]].shape[0]
         low_lanes = lane_tall if height == 128 else lane_deep
         nothing = jnp.zeros((height, 128), jnp.float32)
         pairs = []
-        for b in (first, second):
+        for b in wanted:
             mixed = jnp.where(low_lanes, blocks.get(b + 1, nothing), blocks.get(b - 1, nothing))
             pairs.append(jnp.concatenate([blocks[b], mixed], axis=1))
         high, low = split(jnp.concatenate(pairs, axis=0))
         both = dot(high, col_mats[which])
         flat = both[:, 0:128] + both[:, 128:256] + dot(low, col_mats[which, :, 0:128])
-        return flat[0:height], flat[height : 2 * height]
+        return [flat[height * k : height * (k + 1)] for k in range(len(wanted))]
 
     def along_cols_edge(which, halo):
         high, low = split(halo)
@@ -316,7 +320,7 @@
     pack(0, jnp.where(lane_tall, field[0, 64:192, 0:128], field[0, 64:192, 384:512]))
     pl.semaphore_wait(barrier, expected)
     start(side_copies(0))
-    start(row_copies(0, (0, 1, 2, 3)))
+    start(row_copies(0))
     tell(0)
 
     @pl.when(row == 0)
@@ -386,9 +390,8 @@
     spread(0)
 
     blocks, outs = {}, {}
-    arrive(row_copies(0, (1, 2)))
+    arrive(row_copies(0))
     blocks[1], blocks[2] = pair(along_rows(0, field[0, :, 128:384]))
-    arrive(row_copies(0, (0, 3)))
     blocks[0], blocks[3] = pair(along_rows(0, outer_blocks(field[0])))
     outs[1], outs[2] = along_cols(0, blocks, 1, 2)
     for b in (1, 2):
@@ -437,15 +440,16 @@
     )
     edge = along_cols_edge(1, jnp.where(lane_deep, blocks[4], blocks[-1]))
     outs[-1], outs[4] = along_cols(1, blocks, -1, 4)
-    field[1, :, at(0)] = field[0, :, at(0)] * jnp.where(lane_deep, outs[0] + edge, outs[0])
-    field[1, :, at(3)] = field[0, :, at(3)] * jnp.where(lane_deep, outs[3], outs[3] + edge)
+    first = field[0, :, at(0)] * jnp.where(lane_deep, outs[0] + edge, outs[0])
+    fourth = field[0, :, at(3)] * jnp.where(lane_deep, outs[3], outs[3] + edge)
+    field[1, :, at(0)] = first
+    field[1, :, at(3)] = fourth
     halo = beside[...] * jnp.where(lane_deep, outs[4], outs[-1])
 
-    again[0], again[3] = pair(along_rows(0, outer_blocks(field[1])))
-    again[-1] = again[4] = along_rows(0, halo)
-    outs = {}
-    outs[0], outs[3] = along_cols(0, again, 0, 3)
-    outs[1], outs[2] = along_cols(0, again, 1, 2)
+    both = along_rows(0, jnp.concatenate([first, fourth, halo], axis=1))
+    again[0], again[3] = pair(both)
+    again[-1] = again[4] = both[:, 256:384]
+    outs = along_cols(0, again, 0, 1, 2, 3)
     last_norm = sum(squares(seen[:, at(b)] - outs[b]) for b in range(4))
     last_norm = last_norm + pltpu.roll(last_norm, 64, 1)
     partial[...] = jnp.where(lane[0:1], first_norm, last_norm)
@@ -465,7 +469,7 @@
         field[2, 64:192, at(b)] = seen[:, at(b)] / outs[b]
     pack(1, jnp.where(lane_tall, field[2, 64:192, at(0)], field[2, 64:192, at(3)]))
     start(side_copies(1))
-    start(row_copies(1, (0, 1, 2, 3)))
+    start(row_copies(1))
 
     wait_all(gather_rows, rows - 1, norm_recv.at[0])
     total = gather_rows[0]
@@ -476,7 +480,7 @@
     lax.fori_loop(1, cols, start_norm_col, 0)
 
     blocks, outs = {}, {}
-    arrive(row_copies(1, (0, 1, 2, 3)))
+    arrive(row_copies(1))
     blocks[1], blocks[2] = pair(along_rows(1, field[2, :, 128:384]))
     blocks[0], blocks[3] = pair(along_rows(1, outer_blocks(field[2])))
     outs[1], outs[2] = along_cols(1, blocks, 1, 2)
@@ -490,7 +494,7 @@
     store.start()
     for turn in range(2):
         depart(side_copies(turn))
-        depart(row_copies(turn, (0, 1, 2, 3)))
+        depart(row_copies(turn))
     depart(deep_side_copies())
     depart(deep_row_copies((0, 1, 2, 3)))
     wait_all(gather_rows, rows - 1, norm_send.at[0])

time: 41.7 us -> 41.9 us (level)
  no operation moved by 1% of the time
where the time goes in v6:
time: 41.9 us; the launch traced here: 41.3 us
  Pallas kernels  40 us (95%)
  local copies, waits for them, and re-layouts  0.66 us (2%)
  between operations  0.66 us (2%)
    pallas_call x1, Pallas kernels, body(): pl.pallas_call(functools.partial(kernel, rows, cols), out_shape=(jax.Shap...  39.2 us

profile of v6, /device:TPU:1, one launch (start us, length us, event | category | flops | bytes accessed | tf_op | source)
XLA Modules:
  0.0 41.3 jit_solution(2201270589038270244)
XLA Ops:
  0.6 0.0 copy-start
  0.6 0.0 copy-start.1
  0.7 0.6 %copy-done = f32[127]{0:T(128)S(1)} copy-done((f32[127]{0:T(128)S(1)}, f32[127]{0:T(128)}, u32[]{:S(2)}) %copy-start) | copy-done | bytes 532
  1.3 0.0 copy-done.1
  1.3 39.2 %deconvolve.1 = (f32[128,512]{1,0:T(8,128)S(1)}, f32[1,2]{1,0:T(1,128)S(1)}) custom-call(f32[128,512]{1,0:T(8,128)} %bitcast.8, f32[128,512]{1,0:T(8,128)} %bitcast.9, f32[1,127]{1,0:T(1,128)S(1)} %bitcast.6, f32[1,127]{1,0:T(1,128)S(1)} %bitcast.7), custom_call_target="tpu_custom_call" | custom-call | tf_op jit(solution)/shard_map/deconvolve/pallas_call | solution.py:557
  40.5 0.7 %finish.1 = (f32[128,512]{1,0:T(8,128)}, f32[1,2]{1,0:T(1,128)}) custom-call(f32[128,512]{1,0:T(8,128)S(1)} %get-tuple-element.6.estimate, f32[1,2]{1,0:T(1,128)S(1)} %get-tuple-element.7.norms), custom_call_target="tpu_custom_call" | custom-call | tf_op jit(solution)/shard_map/finish/pallas_call | solution.py:609
Async XLA Ops:
  0.6 0.7 %copy-start = (f32[127]{0:T(128)S(1)}, f32[127]{0:T(128)}, u32[]{:S(2)}) copy-start(f32[127]{0:T(128)} %param.6) | copy-start | bytes 1528
  0.6 0.7 %copy-start.1 = (f32[127]{0:T(128)S(1)}, f32[127]{0:T(128)}, u32[]{:S(2)}) copy-start(f32[127]{0:T(128)} %param.7) | copy-start | bytes 1528

commit v7 on v5

--- a/solution.py
+++ b/solution.py
@@ -389,6 +389,7 @@
     arrive(row_copies(0, (1, 2)))
     blocks[1], blocks[2] = pair(along_rows(0, field[0, :, 128:384]))
     arrive(row_copies(0, (0, 3)))
+    spread(1)
     blocks[0], blocks[3] = pair(along_rows(0, outer_blocks(field[0])))
     outs[1], outs[2] = along_cols(0, blocks, 1, 2)
     for b in (1, 2):
@@ -403,7 +404,6 @@
     inner_sum = inner_sum + squares(
         jnp.where(lane_tall, seen[:, at(3)] - outs[3], seen[:, at(0)] - outs[0])
     )
-    spread(1)
     arrive(side_copies(0))
     halo = sides(0)
     beside[...] = halo

time: 41.7 us -> 41.7 us (level)
  no operation moved by 1% of the time
where the time goes in v7:
time: 41.7 us; the launch traced here: 40.9 us
  Pallas kernels  39.6 us (95%)
  local copies, waits for them, and re-layouts  0.66 us (2%)
  between operations  0.66 us (2%)
    pallas_call x1, Pallas kernels, body(): pl.pallas_call(functools.partial(kernel, rows, cols), out_shape=(jax.Shap...  38.9 us

profile of v7, /device:TPU:1, one launch (start us, length us, event | category | flops | bytes accessed | tf_op | source)
XLA Modules:
  0.0 40.9 jit_solution(14699721417703719466)
XLA Ops:
  0.6 0.0 copy-start
  0.6 0.0 copy-start.1
  0.7 0.6 %copy-done = f32[127]{0:T(128)S(1)} copy-done((f32[127]{0:T(128)S(1)}, f32[127]{0:T(128)}, u32[]{:S(2)}) %copy-start) | copy-done | bytes 532
  1.3 0.0 copy-done.1
  1.3 38.9 %deconvolve.1 = (f32[128,512]{1,0:T(8,128)S(1)}, f32[1,2]{1,0:T(1,128)S(1)}) custom-call(f32[128,512]{1,0:T(8,128)} %bitcast.8, f32[128,512]{1,0:T(8,128)} %bitcast.9, f32[1,127]{1,0:T(1,128)S(1)} %bitcast.6, f32[1,127]{1,0:T(1,128)S(1)} %bitcast.7), custom_call_target="tpu_custom_call" | custom-call | tf_op jit(solution)/shard_map/deconvolve/pallas_call | solution.py:553
  40.2 0.7 %finish.1 = (f32[128,512]{1,0:T(8,128)}, f32[1,2]{1,0:T(1,128)}) custom-call(f32[128,512]{1,0:T(8,128)S(1)} %get-tuple-element.6.estimate, f32[1,2]{1,0:T(1,128)S(1)} %get-tuple-element.7.norms), custom_call_target="tpu_custom_call" | custom-call | tf_op jit(solution)/shard_map/finish/pallas_call | solution.py:605
Async XLA Ops:
  0.6 0.7 %copy-start = (f32[127]{0:T(128)S(1)}, f32[127]{0:T(128)}, u32[]{:S(2)}) copy-start(f32[127]{0:T(128)} %param.6) | copy-start | bytes 1528
  0.6 0.7 %copy-start.1 = (f32[127]{0:T(128)S(1)}, f32[127]{0:T(128)}, u32[]{:S(2)}) copy-start(f32[127]{0:T(128)} %param.7) | copy-start | bytes 1528
